TPU v7x, 32 devices: a whole 2x2x4 slice. The times are simulated.
32 devices in a mesh: frame: 8 (over z, x), batch: 4 (over y, core).
Axes of the slice: x: 2, y: 2, z: 4, core: 2. Of those that a mesh axis runs over, the one named last changes fastest.
Arguments:
- clean: float32 [2, 4, 32, 3, 256], P(None, 'batch', 'frame'), may hold values from -6 to 6
- noise: float32 [2, 4, 32, 3, 256], P(None, 'batch', 'frame'), may hold values from -6 to 6
- timesteps: int32 [2, 4, 1], replicated, may hold values from 0 to 999
- frame_counts: int32 [2, 4, 1], replicated, may hold values from 8 to 32, as said below
- conv_weight: float32 [9216, 256], P('frame', 'batch'), may hold values from -0.125 to 0.125
- conv_first: float32 [9216, 256], P('frame', 'batch'), may hold values from -1.9073486e-05 to 1.9073486e-05
- conv_second: float32 [9216, 256], P('frame', 'batch'), may hold values from 3.9805537e-13 to 6.634256e-12
- proj_in: float32 [512, 768], P('frame', 'batch'), may hold values from -0.375 to 0.375
- proj_in_first: float32 [512, 768], P('frame', 'batch'), may hold values from -1.9073486e-05 to 1.9073486e-05
- proj_in_second: float32 [512, 768], P('frame', 'batch'), may hold values from 3.9805537e-13 to 6.634256e-12
- proj_out: float32 [512, 256], P('frame', 'batch'), may hold values from -1 to 1
- proj_out_first: float32 [512, 256], P('frame', 'batch'), may hold values from -1.9073486e-05 to 1.9073486e-05
- proj_out_second: float32 [512, 256], P('frame', 'batch'), may hold values from 3.9805537e-13 to 6.634256e-12
- time_weight: float32 [512, 256], P('frame', 'batch'), may hold values from -0.375 to 0.375
- time_first: float32 [512, 256], P('frame', 'batch'), may hold values from -1.9073486e-05 to 1.9073486e-05
- time_second: float32 [512, 256], P('frame', 'batch'), may hold values from 3.9805537e-13 to 6.634256e-12
- in_weight: float32 [3, 256], replicated, may hold values from -3.5 to 3.5
- in_first: float32 [3, 256], replicated, may hold values from -0.00012207031 to 0.00012207031
- in_second: float32 [3, 256], replicated, may hold values from 1.4648438e-12 to 2.4414063e-11
- out_weight: float32 [3, 256], replicated, may hold values from -0.375 to 0.375
- out_first: float32 [3, 256], replicated, may hold values from -0.00036621094 to 0.00036621094
- out_second: float32 [3, 256], replicated, may hold values from 1.4648438e-10 to 2.4414062e-09
- gains: float32 [7, 256], replicated, may hold values from 0.4 to 2.6
- gains_first: float32 [7, 256], replicated, may hold values from -0.00012207031 to 0.00012207031
- gains_second: float32 [7, 256], replicated, may hold values from 1.4648438e-12 to 2.4414063e-11
- rel_bias: float32 [4, 32], replicated, may hold values from -4 to 4
- rel_bias_first: float32 [4, 32], replicated, may hold values from -3.8146973e-06 to 3.8146973e-06
- rel_bias_second: float32 [4, 32], replicated, may hold values from 1.4648437e-14 to 2.4414062e-13
Outputs:
- loss_sum: float32 [], replicated
- pixel_count: float32 [], replicated
- grad_norm: float32 [], replicated
- conv_new: float32 [9216, 256], P('frame', 'batch')
- conv_first_new: float32 [9216, 256], P('frame', 'batch')
- conv_second_new: float32 [9216, 256], P('frame', 'batch')
- proj_in_new: float32 [512, 768], P('frame', 'batch')
- proj_in_first_new: float32 [512, 768], P('frame', 'batch')
- proj_in_second_new: float32 [512, 768], P('frame', 'batch')
- proj_out_new: float32 [512, 256], P('frame', 'batch')
- proj_out_first_new: float32 [512, 256], P('frame', 'batch')
- proj_out_second_new: float32 [512, 256], P('frame', 'batch')
- time_new: float32 [512, 256], P('frame', 'batch')
- time_first_new: float32 [512, 256], P('frame', 'batch')
- time_second_new: float32 [512, 256], P('frame', 'batch')
- in_new: float32 [3, 256], replicated
- in_first_new: float32 [3, 256], replicated
- in_second_new: float32 [3, 256], replicated
- out_new: float32 [3, 256], replicated
- out_first_new: float32 [3, 256], replicated
- out_second_new: float32 [3, 256], replicated
- gains_new: float32 [7, 256], replicated
- gains_first_new: float32 [7, 256], replicated
- gains_second_new: float32 [7, 256], replicated
- rel_bias_new: float32 [4, 32], replicated
- rel_bias_first_new: float32 [4, 32], replicated
- rel_bias_second_new: float32 [4, 32], replicated
Inputs may be any that keep to these rules, and one draw needn't show every extreme that they name: `frame_counts`: each value is 8, 16 or 32; in every draw some video has 32 valid frames.
All inputs are finite; a program needn't handle non-finite values.
Results may differ from a plain program's by a relative error of at most 0.012.
The roundings to bfloat16 on the way count: a program that leaves them out, or rounds other values in their place, can miss the bound.
Values may be sent and summed in bfloat16 or wider, within the bound.
A program may use at most 256 MiB of HBM per device.

v0:
```python
import math

import jax
import jax.numpy as jnp
from jax import lax
from jax.sharding import PartitionSpec as P

D = 256
HEADS = 4
FRAMES = 32
SIDE = 16
MICRO = 2
TSTEPS = 1000
STEP = 10


HIGH = lax.Precision.HIGHEST
EPS_NORM = 1e-06
CLIP = 0.05
BETA_ONE = 0.9
BETA_TWO = 0.999
ADAM_EPS = 1e-08
DECAY = 0.01
RATES = (0.02, 0.06, 0.18, 0.06, 0.6, 0.06, 1.0, 1.0)
NEG = -1000000000.0


def swish(values):
    return values * jax.nn.sigmoid(values)


def swish_grad(values):
    sigma_v = jax.nn.sigmoid(values)
    return sigma_v * (1.0 + values * (1.0 - sigma_v))


def norm_fwd(values, gain_vec):
    inverse = lax.rsqrt(jnp.mean(values * values, -1, keepdims=True) + EPS_NORM)
    return (values * inverse * gain_vec, inverse)


def norm_bwd(values, inverse, gain_vec, upstream):
    scaled = upstream * gain_vec
    dvalues = inverse * scaled - values * inverse**3 * jnp.mean(values * scaled, -1, keepdims=True)
    return (dvalues, jnp.sum(upstream * values * inverse, axis=(0, 1)))


def patches(acts):
    frames, pixels, width = acts.shape
    frame_grid = acts.reshape(frames, SIDE, SIDE, width)
    padded = jnp.pad(frame_grid, ((0, 0), (1, 1), (1, 1), (0, 0)))
    columns = [
        padded[:, offset // 3 : offset // 3 + SIDE, offset % 3 : offset % 3 + SIDE]
        for offset in range(9)
    ]
    return jnp.concatenate(columns, -1).reshape(frames * pixels, 9 * width)


def conv_fwd(acts, kernel):
    frames, pixels, width = acts.shape
    return jnp.dot(patches(acts), kernel, preferred_element_type=jnp.float32).reshape(
        frames, pixels, width
    )


def conv_bwd(acts, grad_low, kernel):
    frames, pixels, width = grad_low.shape
    flat_grad = grad_low.reshape(frames * pixels, width)
    dkernel = lax.dot_general(
        patches(acts), flat_grad, (((0,), (0,)), ((), ())), preferred_element_type=jnp.float32
    )
    tap_terms = lax.dot_general(
        flat_grad, kernel, (((1,), (1,)), ((), ())), preferred_element_type=jnp.float32
    )
    padded = jnp.pad(
        tap_terms.reshape(frames, SIDE, SIDE, 9, width), ((0, 0), (1, 1), (1, 1), (0, 0), (0, 0))
    )
    dacts = sum(
        (
            padded[
                :,
                2 - offset // 3 : 2 - offset // 3 + SIDE,
                2 - offset % 3 : 2 - offset % 3 + SIDE,
                offset,
            ]
            for offset in range(9)
        )
    )
    return (dacts.reshape(frames, pixels, width), dkernel)


def res_fwd(hidden, kern_one, kern_two, gain_one, gain_two, frame_bias):
    normed, inverse_one = norm_fwd(hidden, gain_one)
    acts_one = swish(normed).astype(jnp.bfloat16)
    inner_act = conv_fwd(acts_one, kern_one) + frame_bias
    second_norm, inverse_two = norm_fwd(inner_act, gain_two)
    acts_two = swish(second_norm).astype(jnp.bfloat16)
    saved = (normed, inverse_one, acts_one, inner_act, second_norm, inverse_two, acts_two)
    return (hidden + conv_fwd(acts_two, kern_two), saved)


def res_bwd(hidden, upstream, kern_one, kern_two, gain_one, gain_two, saved):
    normed, inverse_one, acts_one, inner_act, second_norm, inverse_two, acts_two = saved
    dacts_two, dkern_two = conv_bwd(acts_two, upstream.astype(jnp.bfloat16), kern_two)
    dinner, dgain_two = norm_bwd(
        inner_act, inverse_two, gain_two, dacts_two * swish_grad(second_norm)
    )
    dacts_one, dkern_one = conv_bwd(acts_one, dinner.astype(jnp.bfloat16), kern_one)
    dhidden, dgain_one = norm_bwd(hidden, inverse_one, gain_one, dacts_one * swish_grad(normed))
    return (upstream + dhidden, dkern_one, dkern_two, dgain_one, dgain_two, jnp.sum(dinner, 1))


def attend_probs(packed, bias_mat, valid):
    batch, length, _ = packed.shape
    split_heads = packed.reshape(batch, length, 3, HEADS, D // HEADS)
    scores = (
        jnp.einsum(
            "blhe,bmhe->bhlm",
            split_heads[:, :, 0],
            split_heads[:, :, 1],
            preferred_element_type=jnp.float32,
        )
        / math.sqrt(D // HEADS)
        + bias_mat
    )
    if valid is not None:
        scores = jnp.where(valid[:, None, None, :], scores, NEG)
    shifted = jnp.exp(scores - jnp.max(scores, -1, keepdims=True))
    return (shifted / jnp.sum(shifted, -1, keepdims=True), split_heads)


def attend_fwd(packed, bias_mat, valid):
    attn_probs, split_heads = attend_probs(packed, bias_mat, valid)
    mixture = jnp.einsum(
        "bhlm,bmhe->blhe",
        attn_probs.astype(jnp.bfloat16),
        split_heads[:, :, 2],
        preferred_element_type=jnp.float32,
    )
    return mixture.reshape(packed.shape[0], packed.shape[1], D).astype(jnp.bfloat16)


def attend_bwd(packed, dmixture, bias_mat, valid):
    batch, length, _ = packed.shape
    attn_probs, split_heads = attend_probs(packed, bias_mat, valid)
    grad_heads = dmixture.reshape(batch, length, HEADS, D // HEADS)
    dattn_probs = jnp.einsum(
        "blhe,bmhe->bhlm", grad_heads, split_heads[:, :, 2], preferred_element_type=jnp.float32
    )
    dvalues = jnp.einsum(
        "bhlm,blhe->bmhe",
        attn_probs.astype(jnp.bfloat16),
        grad_heads,
        preferred_element_type=jnp.float32,
    )
    dscores = attn_probs * (dattn_probs - jnp.sum(attn_probs * dattn_probs, -1, keepdims=True))
    dscore_low = dscores.astype(jnp.bfloat16)
    root_dim = math.sqrt(D // HEADS)
    dquery = (
        jnp.einsum(
            "bhlm,bmhe->blhe", dscore_low, split_heads[:, :, 1], preferred_element_type=jnp.float32
        )
        / root_dim
    )
    dkey_vals = (
        jnp.einsum(
            "bhlm,blhe->bmhe", dscore_low, split_heads[:, :, 0], preferred_element_type=jnp.float32
        )
        / root_dim
    )
    dpacked = (
        jnp.stack([dquery, dkey_vals, dvalues], 2)
        .reshape(batch, length, 3 * D)
        .astype(jnp.bfloat16)
    )
    return (dpacked, jnp.sum(dscores, 0))


def to_rows(spread, videos):
    slots, pix_dev, width = spread.shape
    return (
        spread.reshape(videos, slots // videos, pix_dev, width)
        .transpose(0, 2, 1, 3)
        .reshape(videos * pix_dev, slots // videos, width)
    )


def from_rows(rows, videos):
    count_rows, length, width = rows.shape
    pix_dev = count_rows // videos
    return (
        rows.reshape(videos, pix_dev, length, width)
        .transpose(0, 2, 1, 3)
        .reshape(videos * length, pix_dev, width)
    )


def mixer_fwd(hidden, gain_vec, w_in, w_out, context):
    normed, inverse = norm_fwd(hidden, gain_vec)
    normed_low = normed.astype(jnp.bfloat16)
    packed = jnp.dot(normed_low, w_in, preferred_element_type=jnp.float32).astype(jnp.bfloat16)
    if context is None:
        return (
            hidden
            + jnp.dot(attend_fwd(packed, 0.0, None), w_out, preferred_element_type=jnp.float32),
            (normed_low, inverse, packed, None),
        )
    videos, bias_mat, valid_rows, onehot = context
    spread = lax.all_to_all(packed, "frame", split_axis=1, concat_axis=0, tiled=True)
    mixture = from_rows(attend_fwd(to_rows(spread, videos), bias_mat, valid_rows), videos)
    gathered_back = lax.all_to_all(mixture, "frame", split_axis=0, concat_axis=1, tiled=True)
    return (
        hidden + jnp.dot(gathered_back, w_out, preferred_element_type=jnp.float32),
        (normed_low, inverse, packed, spread),
    )


def mixer_bwd(hidden, upstream, gain_vec, w_in, w_out, context, saved):
    normed_low, inverse, packed, kept_pixels = saved
    grad_low = upstream.astype(jnp.bfloat16)
    dtable_sum = None
    if context is None:
        inputs, grads_out, bias_mat, valid_rows = (packed, grad_low, 0.0, None)
    else:
        videos, bias_mat, valid_rows, onehot = context
        spread, grad_spread = (
            lax.all_to_all(packed, "frame", split_axis=1, concat_axis=0, tiled=True),
            lax.all_to_all(grad_low, "frame", split_axis=1, concat_axis=0, tiled=True),
        )
        inputs, grads_out = (to_rows(spread, videos), to_rows(grad_spread, videos))
    mixture = attend_fwd(inputs, bias_mat, valid_rows)
    dw_out = jnp.einsum("bld,ble->de", mixture, grads_out, preferred_element_type=jnp.float32)
    dmixture = jnp.einsum(
        "ble,de->bld", grads_out, w_out, preferred_element_type=jnp.float32
    ).astype(jnp.bfloat16)
    dpacked, dbias_sum = attend_bwd(inputs, dmixture, bias_mat, valid_rows)
    if context is not None:
        dpacked = lax.all_to_all(
            from_rows(dpacked, videos), "frame", split_axis=0, concat_axis=1, tiled=True
        )
        dtable_sum = jnp.einsum("hlm,lmk->hk", dbias_sum, onehot, precision=HIGH)
    dw_in = jnp.einsum("fpd,fpk->dk", normed_low, dpacked, preferred_element_type=jnp.float32)
    dnormed = jnp.einsum("fpk,dk->fpd", dpacked, w_in, preferred_element_type=jnp.float32)
    dhidden, dgain_vec = norm_bwd(hidden, inverse, gain_vec, dnormed)
    return (upstream + dhidden, dw_in, dw_out, dgain_vec, dtable_sum)


def fetch(conv_weight, proj_in, proj_out, time_weight):
    columns = (
        lax.all_gather(conv_weight.astype(jnp.bfloat16), "batch", axis=1, tiled=True),
        lax.all_gather(proj_in.astype(jnp.bfloat16), "batch", axis=1, tiled=True),
        lax.all_gather(proj_out.astype(jnp.bfloat16), "batch", axis=1, tiled=True),
        lax.all_gather(time_weight.astype(jnp.bfloat16), "batch", axis=1, tiled=True),
    )
    return (
        lax.all_gather(columns[0], "frame", axis=0, tiled=True),
        lax.all_gather(columns[1], "frame", axis=0, tiled=True),
        lax.all_gather(columns[2], "frame", axis=0, tiled=True),
        lax.all_gather(columns[3], "frame", axis=0, tiled=True),
    )


def reduce_rows(matrix_grads):
    row_parts = (
        lax.psum_scatter(matrix_grads[0], "frame", scatter_dimension=0, tiled=True),
        lax.psum_scatter(matrix_grads[1], "frame", scatter_dimension=0, tiled=True),
        lax.psum_scatter(matrix_grads[2], "frame", scatter_dimension=0, tiled=True),
        lax.psum_scatter(matrix_grads[3], "frame", scatter_dimension=0, tiled=True),
    )
    return (
        lax.psum_scatter(row_parts[0], "batch", scatter_dimension=1, tiled=True),
        lax.psum_scatter(row_parts[1], "batch", scatter_dimension=1, tiled=True),
        lax.psum_scatter(row_parts[2], "batch", scatter_dimension=1, tiled=True),
        lax.psum_scatter(row_parts[3], "batch", scatter_dimension=1, tiled=True),
    )


def adamw(weight, moment_one, moment_two, grad, clip_scale, step_rate):
    grad = grad * clip_scale
    moment_one = BETA_ONE * moment_one + (1.0 - BETA_ONE) * grad
    moment_two = BETA_TWO * moment_two + (1.0 - BETA_TWO) * grad * grad
    update = (
        moment_one
        / (1.0 - BETA_ONE**STEP)
        / (jnp.sqrt(moment_two / (1.0 - BETA_TWO**STEP)) + ADAM_EPS)
    )
    return (weight - step_rate * (update + DECAY * weight), moment_one, moment_two)


def shards(
    clean,
    noise,
    timesteps,
    frame_counts,
    conv_weight,
    conv_first,
    conv_second,
    proj_in,
    proj_in_first,
    proj_in_second,
    proj_out,
    proj_out_first,
    proj_out_second,
    time_weight,
    time_first,
    time_second,
    in_weight,
    in_first,
    in_second,
    out_weight,
    out_first,
    out_second,
    gains,
    gains_first,
    gains_second,
    rel_bias,
    rel_bias_first,
    rel_bias_second,
):
    fr_dev = clean.shape[2]
    pixels = clean.shape[4]
    videos = timesteps.shape[2]
    pix_dev = pixels // lax.axis_size("frame")
    group_idx = lax.axis_index("batch")
    frame_ids = lax.axis_index("frame") * fr_dev + jnp.arange(fr_dev)
    member = (frame_ids[:, None] // FRAMES == jnp.arange(videos)[None, :]).astype(jnp.float32)
    frame_place = frame_ids % FRAMES
    pixel_total = jnp.sum(frame_counts).astype(jnp.float32) * pixels
    offsets = jnp.arange(FRAMES)
    distance = offsets[None, :] - offsets[:, None]
    bucket = jnp.minimum(jnp.abs(distance), 15) + 16 * (distance > 0).astype(jnp.int32)
    onehot = (bucket[:, :, None] == jnp.arange(rel_bias.shape[1])[None, None, :]).astype(
        jnp.float32
    )
    bias_mat = jnp.einsum("hk,lmk->hlm", rel_bias, onehot, precision=HIGH)
    half_width = D // 2
    frequency = jnp.exp(-math.log(10000.0) * jnp.arange(half_width, dtype=jnp.float32) / half_width)
    out_low = out_weight.astype(jnp.bfloat16)
    matrix_acc = None
    vector_acc = None
    loss_local = jnp.zeros((), jnp.float32)
    for micro_idx in range(MICRO):
        gathered = fetch(conv_weight, proj_in, proj_out, time_weight)
        kernels = gathered[0].reshape(4, 9 * D, D)
        w_in = gathered[1].reshape(2, D, 3 * D)
        w_out = gathered[2].reshape(2, D, D)
        w_time = gathered[3].reshape(2, D, D)
        steps_grp = lax.dynamic_index_in_dim(timesteps[micro_idx], group_idx, 0, keepdims=False)
        count_grp = lax.dynamic_index_in_dim(frame_counts[micro_idx], group_idx, 0, keepdims=False)
        levels = steps_grp.astype(jnp.float32)
        embedding = jnp.concatenate(
            [jnp.sin(levels[:, None] * frequency), jnp.cos(levels[:, None] * frequency)], -1
        ).astype(jnp.bfloat16)
        time_pre = jnp.einsum("vd,jde->jve", embedding, w_time, preferred_element_type=jnp.float32)
        frame_bias = jnp.einsum("fv,jvd->jfd", member, swish(time_pre), precision=HIGH)[
            :, :, None, :
        ]
        frame_level = jnp.dot(member, levels, precision=HIGH)
        alpha_bar = jnp.cos(0.5 * math.pi * (frame_level + 1.0) / (TSTEPS + 1.0)) ** 2
        target = noise[micro_idx, 0]
        noisy_input = (
            jnp.sqrt(alpha_bar)[:, None, None] * clean[micro_idx, 0]
            + jnp.sqrt(1.0 - alpha_bar)[:, None, None] * target
        )
        frame_count = jnp.sum(member * count_grp.astype(jnp.float32)[None, :], 1)
        live_frames = (frame_place.astype(jnp.float32) < frame_count).astype(jnp.float32)
        valid_video = offsets[None, :] < count_grp[:, None]
        valid_rows = jnp.broadcast_to(valid_video[:, None, :], (videos, pix_dev, FRAMES)).reshape(
            videos * pix_dev, FRAMES
        )
        context = (videos, bias_mat, valid_rows, onehot)
        hidden_zero = jnp.einsum("fcp,cd->fpd", noisy_input, in_weight, precision=HIGH)
        hidden_one, saved_zero = res_fwd(
            hidden_zero, kernels[0], kernels[1], gains[0], gains[1], frame_bias[0]
        )
        hidden_two, saved_spatial = mixer_fwd(hidden_one, gains[2], w_in[0], w_out[0], None)
        hidden_three, saved_temporal = mixer_fwd(hidden_two, gains[3], w_in[1], w_out[1], context)
        hidden_four, saved_last = res_fwd(
            hidden_three, kernels[2], kernels[3], gains[4], gains[5], frame_bias[1]
        )
        normed, inverse = norm_fwd(hidden_four, gains[6])
        normed_low = normed.astype(jnp.bfloat16)
        predicted = jnp.einsum(
            "fpd,cd->fcp", normed_low, out_low, preferred_element_type=jnp.float32
        )
        pred_error = predicted - target
        weighted = live_frames[:, None, None] * pred_error
        loss_local = loss_local + jnp.sum(weighted * pred_error)
        dpred = 2.0 * weighted / pixel_total
        d_out = jnp.einsum("fcp,fpd->cd", dpred, normed_low.astype(jnp.float32), precision=HIGH)
        dnormed = jnp.einsum("fcp,cd->fpd", dpred, out_low.astype(jnp.float32), precision=HIGH)
        dhid_four, dgain_six = norm_bwd(hidden_four, inverse, gains[6], dnormed)
        dhid_three, dkern_two, dkern_three, dgain_four, dgain_five, dbias_one = res_bwd(
            hidden_three, dhid_four, kernels[2], kernels[3], gains[4], gains[5], saved_last
        )
        dhid_two, din_one, dout_one, dgain_three, dtable = mixer_bwd(
            hidden_two, dhid_three, gains[3], w_in[1], w_out[1], context, saved_temporal
        )
        dhid_one, din_zero, dout_zero, dgain_two, _ = mixer_bwd(
            hidden_one, dhid_two, gains[2], w_in[0], w_out[0], None, saved_spatial
        )
        dhid_zero, dkern_zero, dkern_one, dgain_zero, dgain_one, dbias_zero = res_bwd(
            hidden_zero, dhid_one, kernels[0], kernels[1], gains[0], gains[1], saved_zero
        )
        dtime_pre = jnp.einsum(
            "fv,jfd->jvd", member, jnp.stack([dbias_zero, dbias_one]), precision=HIGH
        ) * swish_grad(time_pre)
        dtime = jnp.einsum("vd,jve->jde", embedding.astype(jnp.float32), dtime_pre, precision=HIGH)
        d_in = jnp.einsum("fcp,fpd->cd", noisy_input, dhid_zero, precision=HIGH)
        matrix_grads = (
            jnp.stack([dkern_zero, dkern_one, dkern_two, dkern_three]).reshape(36 * D, D),
            jnp.stack([din_zero, din_one]).reshape(2 * D, 3 * D),
            jnp.stack([dout_zero, dout_one]).reshape(2 * D, D),
            dtime.reshape(2 * D, D),
        )
        vector_grads = (
            d_in,
            d_out,
            jnp.stack(
                [dgain_zero, dgain_one, dgain_two, dgain_three, dgain_four, dgain_five, dgain_six]
            ),
            dtable,
        )
        matrix_acc = (
            matrix_grads if matrix_acc is None else jax.tree.map(jnp.add, matrix_acc, matrix_grads)
        )
        vector_acc = (
            vector_grads if vector_acc is None else jax.tree.map(jnp.add, vector_acc, vector_grads)
        )
    matrix_acc = reduce_rows(matrix_acc)
    sum_in, sum_out, sum_gains, sum_table, loss_sum = lax.psum(
        (vector_acc[0], vector_acc[1], vector_acc[2], vector_acc[3], loss_local), ("frame", "batch")
    )
    local_square = sum((jnp.sum(grad * grad) for grad in matrix_acc))
    square = lax.psum(local_square, ("frame", "batch")) + sum(
        (jnp.sum(grad * grad) for grad in (sum_in, sum_out, sum_gains, sum_table))
    )
    grad_norm = jnp.sqrt(square)
    clip_scale = CLIP / jnp.maximum(grad_norm, CLIP)
    conv_new, conv_first_new, conv_second_new = adamw(
        conv_weight, conv_first, conv_second, matrix_acc[0], clip_scale, RATES[0]
    )
    pin_new, pin_first_new, pin_second_new = adamw(
        proj_in, proj_in_first, proj_in_second, matrix_acc[1], clip_scale, RATES[1]
    )
    pout_new, pout_first_new, pout_second_new = adamw(
        proj_out, proj_out_first, proj_out_second, matrix_acc[2], clip_scale, RATES[2]
    )
    time_new, time_first_new, time_second_new = adamw(
        time_weight, time_first, time_second, matrix_acc[3], clip_scale, RATES[3]
    )
    in_new, in_first_new, in_second_new = adamw(
        in_weight, in_first, in_second, sum_in, clip_scale, RATES[4]
    )
    out_new, out_first_new, out_second_new = adamw(
        out_weight, out_first, out_second, sum_out, clip_scale, RATES[5]
    )
    gains_new, gains_first_new, gains_second_new = adamw(
        gains, gains_first, gains_second, sum_gains, clip_scale, RATES[6]
    )
    bias_new, bias_first_new, bias_second_new = adamw(
        rel_bias, rel_bias_first, rel_bias_second, sum_table, clip_scale, RATES[7]
    )
    return (
        loss_sum,
        pixel_total,
        grad_norm,
        conv_new,
        conv_first_new,
        conv_second_new,
        pin_new,
        pin_first_new,
        pin_second_new,
        pout_new,
        pout_first_new,
        pout_second_new,
        time_new,
        time_first_new,
        time_second_new,
        in_new,
        in_first_new,
        in_second_new,
        out_new,
        out_first_new,
        out_second_new,
        gains_new,
        gains_first_new,
        gains_second_new,
        bias_new,
        bias_first_new,
        bias_second_new,
    )


def solution(mesh):
    in_specs = (
        P(None, "batch", "frame", None, None),
        P(None, "batch", "frame", None, None),
        P(),
        P(),
        P("frame", "batch"),
        P("frame", "batch"),
        P("frame", "batch"),
        P("frame", "batch"),
        P("frame", "batch"),
        P("frame", "batch"),
        P("frame", "batch"),
        P("frame", "batch"),
        P("frame", "batch"),
        P("frame", "batch"),
        P("frame", "batch"),
        P("frame", "batch"),
        P(),
        P(),
        P(),
        P(),
        P(),
        P(),
        P(),
        P(),
        P(),
        P(),
        P(),
        P(),
    )
    out_specs = (
        P(),
        P(),
        P(),
        P("frame", "batch"),
        P("frame", "batch"),
        P("frame", "batch"),
        P("frame", "batch"),
        P("frame", "batch"),
        P("frame", "batch"),
        P("frame", "batch"),
        P("frame", "batch"),
        P("frame", "batch"),
        P("frame", "batch"),
        P("frame", "batch"),
        P("frame", "batch"),
        P(),
        P(),
        P(),
        P(),
        P(),
        P(),
        P(),
        P(),
        P(),
        P(),
        P(),
        P(),
    )
    return jax.shard_map(shards, mesh=mesh, in_specs=in_specs, out_specs=out_specs, check_vma=False)
```

profile of v0, /device:TPU:0, one launch (start us, length us, event | category | flops | bytes accessed | tf_op | source)
XLA Modules:
  0.0 1082.2 jit_solution(9757178318866104448)
XLA Ops:
  8.3 9.0 all_gather.32
  49.7 32.5 %all_gather.39 = bf16[512,256]{1,0:T(8,128)(2,1)S(1)} all-gather(bf16[64,256]{1,0:T(8,128)(2,1)S(1)} %copy.333), channel_id=1, replica_groups=mesh['frame'=8,'batch'=4] {'frame'}, dimensions={0}, use_global_device_ids=true | all-gather | bytes 294912 | tf_op jit(solution)/shard_map/all_gather | solution.py:258
  82.2 31.3 %all_gather.35 = bf16[512,256]{1,0:T(8,128)(2,1)S(1)} all-gather(bf16[64,256]{1,0:T(8,128)(2,1)S(1)} %copy.325), channel_id=1, replica_groups=mesh['frame'=8,'batch'=4] {'frame'}, dimensions={0}, use_global_device_ids=true | all-gather | bytes 294912 | tf_op jit(solution)/shard_map/all_gather | solution.py:259
  115.5 5.4 all-gather
  135.2 32.3 %all_gather.37 = bf16[512,768]{1,0:T(8,128)(2,1)S(1)} all-gather(bf16[64,768]{1,0:T(8,128)(2,1)S(1)} %bitcast.1113), channel_id=1, replica_groups=mesh['frame'=8,'batch'=4] {'frame'}, dimensions={0}, use_global_device_ids=true | all-gather | bytes 884736 | tf_op jit(solution)/shard_map/all_gather | solution.py:257
  199.1 5.6 all-to-all-start.2
  236.5 6.0 all-to-all-start
  261.4 5.7 reshape.1302
  267.1 5.4 fusion.284
  272.4 5.5 fusion.296
  284.9 6.2 all-to-all-start.3
  294.1 5.7 reshape.1301
  299.8 5.3 fusion.285
  319.3 6.0 all-to-all-start.1
  392.7 6.0 all-to-all-start.4
  429.6 6.2 all-to-all-start.6
  450.0 5.7 convert_element_type.386
  459.3 6.3 all-to-all-start.5
  486.9 5.7 convert_element_type.398
  496.1 6.0 all-to-all-start.7
  508.2 5.4 convolution_bitcast_fusion
  513.7 5.3 convolution_bitcast_fusion.4
  528.3 6.4 all-to-all-done.7
  605.8 9.6 copy.392
  623.3 58.5 %reduce-scatter.23.cloned.1.call-done = f32[64,256]{1,0:T(8,128)} async-done(((f32[512,256]{1,0:T(8,128)}), f32[64,256]{1,0:T(8,128)}) %reduce-scatter.23.cloned.1.call-update) | async-done | bytes 65552 | tf_op jit(solution)/shard_map/reduce_scatter | solution.py:268
  683.5 6.2 fusion.310
  689.7 59.4 %reduce-scatter.19.cloned.1.call-done = f32[64,768]{1,0:T(8,128)} async-done(((f32[512,768]{1,0:T(8,128)}), f32[64,768]{1,0:T(8,128)}) %reduce-scatter.19.cloned.1.call-update) | async-done | bytes 196624 | tf_op jit(solution)/shard_map/reduce_scatter | solution.py:266
  756.3 158.9 %reduce-scatter.15.cloned.1.call-done = f32[1152,256]{0,1:T(8,128)} async-done(((f32[9216,256]{0,1:T(8,128)}), f32[1152,256]{0,1:T(8,128)}) %reduce-scatter.15.cloned.1.call-update) | async-done | bytes 1179664 | tf_op jit(solution)/shard_map/reduce_scatter | solution.py:265
  937.8 21.8 %reduce-scatter.29.cloned.1.call-done = f32[64,64]{1,0:T(8,128)} async-done(((f32[256,64]{1,0:T(8,128)}), f32[64,64]{1,0:T(8,128)}) %reduce-scatter.29.cloned.1.call-update) | async-done | bytes 16400
  961.6 21.4 %reduce-scatter.25.cloned.1.call-done = f32[192,64]{1,0:T(8,128)} async-done(((f32[768,64]{1,0:T(8,128)}), f32[192,64]{1,0:T(8,128)}) %reduce-scatter.25.cloned.1.call-update) | async-done | bytes 49168
  984.6 26.9 %reduce-scatter.17.cloned.1.call-done = f32[1152,64]{0,1:T(8,128)} async-done(((f32[1152,256]{0,1:T(8,128)}), f32[1152,64]{0,1:T(8,128)}) %reduce-scatter.17.cloned.1.call-update) | async-done | bytes 294928 | tf_op jit(solution)/shard_map/reduce_scatter | solution.py:271
  1015.7 39.9 %all-reduce.16 = (f32[]{:T(128)}, f32[]{:T(128)}, f32[3,256]{1,0:T(4,128)S(1)}, f32[3,256]{1,0:T(4,128)S(1)}, f32[7,256]{1,0:T(8,128)S(1)}, /*index=5*/f32[4,32]{1,0:T(4,128)S(1)}) all-reduce(f32[]{:T(128)S(6)} %add.1026, f32[]{:T(128)S(6)} %add.1106, ...), channel_id=1, replica_groups=mesh['frame'=8,'batch'=4] {'frame','batch'}, use_global_device_ids=true, to_apply=%region_24.25 | all-reduce | flops 3458 | bytes 27664 | tf_op jit(solution)/shard_map/psum | solution.py:431
  (962 shorter events, 436.0 us)
Async XLA Ops:
  7.2 114.6 %copy-start.221 = (f32[3,256]{1,0:T(4,128)S(1)}, f32[3,256]{1,0:T(4,128)}, u32[]{:S(2)}) copy-start(f32[3,256]{1,0:T(4,128)} %param.44) | copy-start | bytes 9220
  7.2 117.2 %copy-start.223 = (f32[7,256]{1,0:T(8,128)S(1)}, f32[7,256]{1,0:T(8,128)}, u32[]{:S(2)}) copy-start(f32[7,256]{1,0:T(8,128)} %param.50) | copy-start | bytes 21508
  7.2 160.2 %all-gather.3.cloned.1.call-start = ((), (), s32[]{:S(2)}) async-start(), calls=%async_computation.16 | async-start | bytes 5308416 | tf_op jit(solution)/shard_map/all_gather | solution.py:256
  21.1 94.4 %copy-start.240 = (f32[4]{0:T(128)}, f32[4]{0:T(128)S(1)}, u32[]{:S(2)}) copy-start(f32[4]{0:T(128)S(1)} %get-tuple-element.316) | copy-start | bytes 52
  21.1 94.4 %copy-start.241 = (f32[4]{0:T(128)}, f32[4]{0:T(128)S(1)}, u32[]{:S(2)}) copy-start(f32[4]{0:T(128)S(1)} %get-tuple-element.317) | copy-start | bytes 52
  23.1 100.7 %copy-start.242 = (f32[4]{0:T(128)}, f32[4]{0:T(128)S(1)}, u32[]{:S(2)}) copy-start(f32[4]{0:T(128)S(1)} %get-tuple-element.318) | copy-start | bytes 52
  23.1 103.1 %copy-start.243 = (f32[4]{0:T(128)}, f32[4]{0:T(128)S(1)}, u32[]{:S(2)}) copy-start(f32[4]{0:T(128)S(1)} %get-tuple-element.319) | copy-start | bytes 52
  25.1 90.4 %copy-start.237 = (s32[32,32]{1,0:T(8,128)}, s32[32,32]{1,0:T(8,128)S(1)}, u32[]{:S(2)}) copy-start(s32[32,32]{1,0:T(8,128)S(1)} %select_add_fusion) | copy-start | bytes 12292
  34.9 91.3 %copy-start.182 = (f32[1,1,4,3,256]{4,2,3,1,0:T(4,128)}, f32[1,1,4,3,256]{4,2,3,1,0:T(4,128)S(1)}, u32[]{:S(2)}) copy-start(f32[1,1,4,3,256]{4,2,3,1,0:T(4,128)S(1)} %get-tuple-element.188) | copy-start | bytes 36868
  125.0 88.1 %copy-start.217 = (f32[1,256]{1,0:T(1,128)}, f32[1,256]{1,0:T(1,128)S(1)}, u32[]{:S(2)}) copy-start(f32[1,256]{1,0:T(1,128)S(1)} %get-tuple-element.197) | copy-start | bytes 3076
  125.0 100.9 %copy-start.219 = (f32[1,256]{1,0:T(1,128)}, f32[1,256]{1,0:T(1,128)S(1)}, u32[]{:S(2)}) copy-start(f32[1,256]{1,0:T(1,128)S(1)} %get-tuple-element.196) | copy-start | bytes 3076
  199.1 37.4 %all-to-all-start.2 = ((bf16[4,256,768]{2,0,1:T(4,128)(2,1)}), bf16[4,256,768]{2,0,1:T(4,128)(2,1)}, u32[]{:S(2)}, u32[]{:S(2)}) async-start(bf16[4,256,768]{2,0,1:T(4,128)(2,1)} %copy.355), calls=%async_computation.2 | async-start | bytes 3145728 | tf_op jit(solution)/shard_map/all_to_all | solution.py:209
  236.5 48.4 %all-to-all-start = ((bf16[4,256,768]{2,0,1:T(4,128)(2,1)}), bf16[4,256,768]{2,0,1:T(4,128)(2,1)}, u32[]{:S(2)}, u32[]{:S(2)}) async-start(bf16[4,256,768]{2,0,1:T(4,128)(2,1)} %copy.335), calls=%async_computation | async-start | bytes 3145728 | tf_op jit(solution)/shard_map/all_to_all | solution.py:209
  284.9 34.4 %all-to-all-start.3 = ((bf16[32,32,256]{2,1,0:T(8,128)(2,1)}), bf16[32,32,256]{2,1,0:T(8,128)(2,1)}, u32[]{:S(2)}, u32[]{:S(2)}) async-start(bf16[32,32,256]{2,1,0:T(8,128)(2,1)} %copy.364), calls=%async_computation.3 | async-start | bytes 1048576 | tf_op jit(solution)/shard_map/all_to_all | solution.py:211
  319.3 19.6 %all-to-all-start.1 = ((bf16[32,32,256]{2,1,0:T(8,128)(2,1)}), bf16[32,32,256]{2,1,0:T(8,128)(2,1)}, u32[]{:S(2)}, u32[]{:S(2)}) async-start(bf16[32,32,256]{2,1,0:T(8,128)(2,1)} %copy.345), calls=%async_computation.1 | async-start | bytes 1048576 | tf_op jit(solution)/shard_map/all_to_all | solution.py:211
  392.7 36.9 %all-to-all-start.4 = ((bf16[4,256,256]{2,0,1:T(4,128)(2,1)}), bf16[4,256,256]{2,0,1:T(4,128)(2,1)}, u32[]{:S(2)}, u32[]{:S(2)}) async-start(bf16[4,256,256]{2,0,1:T(4,128)(2,1)} %copy.366), calls=%async_computation.4 | async-start | bytes 1048576 | tf_op jit(solution)/shard_map/all_to_all | solution.py:228
  429.6 29.7 %all-to-all-start.6 = ((bf16[4,256,256]{2,0,1:T(4,128)(2,1)}), bf16[4,256,256]{2,0,1:T(4,128)(2,1)}, u32[]{:S(2)}, u32[]{:S(2)}) async-start(bf16[4,256,256]{2,0,1:T(4,128)(2,1)} %copy.379), calls=%async_computation.6 | async-start | bytes 1048576 | tf_op jit(solution)/shard_map/all_to_all | solution.py:228
  459.3 36.8 %all-to-all-start.5 = ((bf16[32,32,768]{2,1,0:T(8,128)(2,1)}), bf16[32,32,768]{2,1,0:T(8,128)(2,1)}, u32[]{:S(2)}, u32[]{:S(2)}) async-start(bf16[32,32,768]{2,1,0:T(8,128)(2,1)} %copy.372), calls=%async_computation.5 | async-start | bytes 3145728 | tf_op jit(solution)/shard_map/all_to_all | solution.py:238
  496.1 38.6 %all-to-all-start.7 = ((bf16[32,32,768]{2,1,0:T(8,128)(2,1)}), bf16[32,32,768]{2,1,0:T(8,128)(2,1)}, u32[]{:S(2)}, u32[]{:S(2)}) async-start(bf16[32,32,768]{2,1,0:T(8,128)(2,1)} %copy.385), calls=%async_computation.7 | async-start | bytes 3145728 | tf_op jit(solution)/shard_map/all_to_all | solution.py:238
  502.1 118.5 %reduce-scatter.21.cloned.1.call-start = ((), (), s32[]{:S(2)}) async-start(), calls=%async_computation.20 | async-start | bytes 589824 | tf_op jit(solution)/shard_map/reduce_scatter | solution.py:267
  556.5 125.3 %reduce-scatter.23.cloned.1.call-start = ((), (), s32[]{:S(2)}) async-start(), calls=%async_computation.21 | async-start | bytes 589824 | tf_op jit(solution)/shard_map/reduce_scatter | solution.py:268
  580.1 169.0 %reduce-scatter.19.cloned.1.call-start = ((), (), s32[]{:S(2)}) async-start(), calls=%async_computation.19 | async-start | bytes 1769472 | tf_op jit(solution)/shard_map/reduce_scatter | solution.py:266
  586.9 328.3 %reduce-scatter.15.cloned.1.call-start = ((), (), s32[]{:S(2)}) async-start(), calls=%async_computation.17 | async-start | bytes 10616832 | tf_op jit(solution)/shard_map/reduce_scatter | solution.py:265
  615.5 321.4 %reduce-scatter.27.cloned.1.call-start = ((), (), s32[]{:S(2)}) async-start(), calls=%async_computation.23 | async-start | bytes 163840
  622.2 337.3 %reduce-scatter.29.cloned.1.call-start = ((), (), s32[]{:S(2)}) async-start(), calls=%async_computation.24 | async-start | bytes 163840
  683.4 299.6 %reduce-scatter.25.cloned.1.call-start = ((), (), s32[]{:S(2)}) async-start(), calls=%async_computation.22 | async-start | bytes 491520
  751.0 260.5 %reduce-scatter.17.cloned.1.call-start = ((), (), s32[]{:S(2)}) async-start(), calls=%async_computation.18 | async-start | bytes 1474560 | tf_op jit(solution)/shard_map/reduce_scatter | solution.py:271
  926.3 137.7 %copy-start.222 = (f32[3,256]{1,0:T(4,128)S(1)}, f32[3,256]{1,0:T(4,128)}, u32[]{:S(2)}) copy-start(f32[3,256]{1,0:T(4,128)} %param.44) | copy-start | bytes 9220
  926.3 143.3 %copy-start.177 = (f32[64,192]{1,0:T(8,128)S(1)}, f32[64,192]{1,0:T(8,128)}, u32[]{:S(2)}) copy-start(f32[64,192]{1,0:T(8,128)} %param.35) | copy-start | bytes 147460
  926.3 144.8 %copy-start.169 = (f32[1152,64]{0,1:T(8,128)S(1)}, f32[1152,64]{0,1:T(8,128)}, u32[]{:S(2)}) copy-start(f32[1152,64]{0,1:T(8,128)} %param.32) | copy-start | bytes 884740
  933.6 137.5 %copy-start.175 = (f32[1152,64]{0,1:T(8,128)S(1)}, f32[1152,64]{0,1:T(8,128)}, u32[]{:S(2)}) copy-start(f32[1152,64]{0,1:T(8,128)} %param.33) | copy-start | bytes 884740
  933.6 137.5 %copy-start.176 = (f32[1152,64]{0,1:T(8,128)S(1)}, f32[1152,64]{0,1:T(8,128)}, u32[]{:S(2)}) copy-start(f32[1152,64]{0,1:T(8,128)} %param.34) | copy-start | bytes 884740
  (245 other events, 1621.3 us)
Sparse Core Ops, SparseCore 0:
  18.5 87.2 all-gather.2
  556.6 60.4 reduce-scatter.20
  620.8 60.9 reduce-scatter.22
  685.1 63.9 reduce-scatter.18
  752.9 162.2 reduce-scatter.14
  918.2 18.6 reduce-scatter.26
  939.9 19.5 reduce-scatter.28
  962.2 20.8 reduce-scatter.24
  985.8 25.7 reduce-scatter.16
where the time goes:
time: 1090 us; the launch traced here: 1080 us
  waiting for transfers between devices  355 us (33%)
  local copies, waits for them, and re-layouts  232 us (21%)
  blocking collectives  161 us (15%)
  matrix products  155 us (14%)
  other arithmetic  102 us (9%)
  starting transfers between devices  49.8 us (5%)
  between operations  28.5 us (3%)
    reduce_scatter x1, waiting for transfers between devices, reduce_rows(): lax.psum_scatter(matrix_grads[0], 'frame', scatter_dimension=0, tiled=True)  159 us
    unnamed x657, local copies, waits for them, and re-layouts  103 us
    reduce_scatter x1, waiting for transfers between devices, reduce_rows(): lax.psum_scatter(matrix_grads[1], 'frame', scatter_dimension=0, tiled=True)  59.4 us
    reduce_scatter x1, waiting for transfers between devices, reduce_rows(): lax.psum_scatter(matrix_grads[3], 'frame', scatter_dimension=0, tiled=True)  58.5 us
    unnamed x12, waiting for transfers between devices  44.4 us
    psum x1, blocking collectives, shards(): lax.psum((vector_acc[0], vector_acc[1], vector_acc[2], vector_acc[3], los...  39.9 us
    all_gather x1, blocking collectives, fetch(): lax.all_gather(columns[2], 'frame', axis=0, tiled=True)  32.5 us
    all_gather x1, blocking collectives, fetch(): lax.all_gather(columns[1], 'frame', axis=0, tiled=True)  32.3 us
  transfers between devices with their start and end apart: 17, of which 9 were waited for; matrix products, arithmetic and copies ran while one was open for 32% of the time, Pallas kernels for 0%

commit v1 on v0

--- a/solution.py
+++ b/solution.py
@@ -3,6 +3,8 @@
 import jax
 import jax.numpy as jnp
 from jax import lax
+from jax.experimental import pallas as pl
+from jax.experimental.pallas import tpu as pltpu
 from jax.sharding import PartitionSpec as P
 
 D = 256
@@ -285,6 +287,1046 @@
         / (jnp.sqrt(moment_two / (1.0 - BETA_TWO**STEP)) + ADAM_EPS)
     )
     return (weight - step_rate * (update + DECAY * weight), moment_one, moment_two)
+
+
+ROW_CONV = 576
+ROW_GRAD = 704
+ROW_ALL = 736
+HALF = 352
+PAIRS = 4
+GAP = 272
+NEVER = -1e30
+MESH_ID = pl.DeviceIdType.MESH
+
+
+def dot_nn(lhs, rhs):
+    return jnp.dot(lhs, rhs, preferred_element_type=jnp.float32)
+
+
+def dot_nt(lhs, rhs):
+    return lax.dot_general(lhs, rhs, (((1,), (1,)), ((), ())), preferred_element_type=jnp.float32)
+
+
+def dot_tn(lhs, rhs):
+    return lax.dot_general(lhs, rhs, (((0,), (0,)), ((), ())), preferred_element_type=jnp.float32)
+
+
+def low(values):
+    return values.astype(jnp.bfloat16)
+
+
+def rms(values, gain_row):
+    inverse = lax.rsqrt(jnp.mean(values * values, -1, keepdims=True) + EPS_NORM)
+    return values * inverse * gain_row, inverse
+
+
+def rms_back(values, inverse, gain_row, upstream):
+    scaled = upstream * gain_row
+    unit = values * inverse
+    mean = jnp.mean(unit * scaled, -1, keepdims=True)
+    return inverse * (scaled - unit * mean), jnp.sum(upstream * unit, 0, keepdims=True)
+
+
+def weave(block):
+    first = block[:256].reshape(32, 1, 8, D)
+    second = block[256:].reshape(32, 1, 8, D)
+    return jnp.concatenate([first, second], 1).reshape(512, D)
+
+
+def unweave(block):
+    parts = block.reshape(32, 2, 8, D)
+    return jnp.concatenate([parts[:, 0].reshape(256, D), parts[:, 1].reshape(256, D)], 0)
+
+
+def tap_pieces(tap):
+    start, stop = 256 * tap, 256 * tap + 256
+    pieces = []
+    while start < stop:
+        block, offset = divmod(start, ROW_CONV)
+        size = min(ROW_CONV - offset, stop - start)
+        pieces.append((block // 2, block % 2, offset, size))
+        start += size
+    return pieces
+
+
+def step_kernel(
+    packed_ref,
+    clip_ref,
+    embed_ref,
+    table_ref,
+    gains_ref,
+    win_ref,
+    wout_ref,
+    headpad_ref,
+    scal_ref,
+    grads_ref,
+    vector_ref,
+    squares_ref,
+    wall,
+    dslab,
+    proj,
+    outp,
+    mine,
+    hid_one,
+    hid_two,
+    inner_zero,
+    dhid,
+    pack_zero,
+    mix_zero,
+    spread_norm,
+    pack_one,
+    prob_one,
+    mix_one,
+    mix_back,
+    dout_pix,
+    dnorm_back,
+    stage,
+    bias_acc,
+    shift_fwd,
+    shift_one,
+    shift_two,
+    act_one,
+    act_two,
+    acc_out,
+    red_sib,
+    red_a,
+    red_b,
+    red_c,
+    red_d,
+    red_z,
+    part_z,
+    final,
+    vec_acc,
+    vec_recv,
+    sq_acc,
+    sq_recv,
+    sem_sib,
+    sem_z,
+    sem_x,
+    sem_y,
+    sem_xf,
+    sem_yf,
+    sem_n,
+    sem_m,
+    sem_dy,
+    sem_dn,
+    sem_red,
+    sem_fin,
+    sem_vec,
+    sem_sq,
+):
+    fr = lax.axis_index("frame")
+    ba = lax.axis_index("batch")
+    z, x = fr // 2, fr % 2
+    y, c = ba // 2, ba % 2
+    ox, oy, oc = 1 - x, 1 - y, 1 - c
+    quarter = 2 * x + c
+    sibling = (fr, 2 * y + oc)
+    x_peer = (2 * z + ox, ba)
+    y_peer = (fr, 2 * oy + c)
+    xs_peer = (2 * z + ox, 2 * y + oc)
+    z_ids = [(z + k) % 4 for k in (1, 2, 3)]
+    z_peers = [(2 * k + x, ba) for k in z_ids]
+    group = [(sibling, 2 * x + oc), (x_peer, 2 * ox + c), (xs_peer, 2 * ox + oc)]
+
+    def remote(src, dst, sems, send_at, recv_at, device):
+        return pltpu.make_async_remote_copy(
+            src_ref=src,
+            dst_ref=dst,
+            send_sem=sems.at[(0,) + send_at],
+            recv_sem=sems.at[(1,) + recv_at],
+            device_id=device,
+            device_id_type=MESH_ID,
+        )
+
+    barrier = pltpu.get_barrier_semaphore()
+    everyone = [sibling, x_peer, y_peer, xs_peer] + z_peers
+    for peer in everyone:
+        pl.semaphore_signal(barrier, inc=1, device_id=peer, device_id_type=MESH_ID)
+    pl.semaphore_wait(barrier, len(everyone))
+
+    first = remote(packed_ref.at[oc], mine, sem_vec, (0,), (0,), sibling)
+    first.start()
+    zeros_row = jnp.zeros((3, 16, D), jnp.bfloat16)
+    for frame in range(9):
+        shift_one[:, GAP * frame : GAP * frame + 16, :] = zeros_row
+        shift_two[:, GAP * frame : GAP * frame + 16, :] = zeros_row
+    for frame in range(3):
+        shift_fwd[:, GAP * frame : GAP * frame + 16, :] = zeros_row
+    bias_acc[...] = jnp.zeros_like(bias_acc)
+    vec_acc[...] = jnp.zeros_like(vec_acc)
+    acc_out[...] = jnp.zeros_like(acc_out)
+    first.wait()
+    wall[y, fr, c] = packed_ref[c] + mine[...]
+
+    own = wall.at[y, fr, c]
+    sends = []
+
+    def go(copy):
+        copy.start()
+        sends.append(copy)
+
+    def arrive(dst, sems, at):
+        remote(dst, dst, sems, at, at, sibling).wait_recv()
+
+    def to_sibling(row_z, row_x, row_y):
+        block = wall.at[row_y, 2 * row_z + row_x, c]
+        at = (row_z, row_x, row_y)
+        go(remote(block, block, sem_sib, at, at, sibling))
+
+    lo, hi = pl.ds(0, 368), pl.ds(368, 368)
+    for k, peer in enumerate(z_peers):
+        go(remote(own, own, sem_z, (k,), (2 - k,), peer))
+    go(remote(own, own, sem_x, (z,), (z,), x_peer))
+    go(remote(own, own, sem_y, (z,), (z,), y_peer))
+    to_sibling(z, x, y)
+    for k, row_z in enumerate(z_ids):
+        block = wall.at[y, 2 * row_z + x, c]
+        arrive(block, sem_z, (k,))
+        go(remote(block, block, sem_x, (row_z,), (row_z,), x_peer))
+        go(remote(block, block, sem_y, (row_z,), (row_z,), y_peer))
+        to_sibling(row_z, x, y)
+    for row_z in [z] + z_ids:
+        block = wall.at[y, 2 * row_z + ox, c]
+        arrive(block, sem_x, (row_z,))
+        part = wall.at[y, 2 * row_z + ox, c, lo]
+        go(remote(part, part, sem_yf, (row_z,), (row_z,), y_peer))
+        to_sibling(row_z, ox, y)
+        block = wall.at[oy, 2 * row_z + x, c]
+        arrive(block, sem_y, (row_z,))
+        part = wall.at[oy, 2 * row_z + x, c, hi]
+        go(remote(part, part, sem_xf, (row_z,), (row_z,), x_peer))
+        to_sibling(row_z, x, oy)
+    for row_z in [z] + z_ids:
+        arrive(wall.at[oy, 2 * row_z + ox, c, lo], sem_yf, (row_z,))
+        arrive(wall.at[oy, 2 * row_z + ox, c, hi], sem_xf, (row_z,))
+        to_sibling(row_z, ox, oy)
+    for row_z in range(4):
+        for row_x in range(2):
+            for row_y in range(2):
+                arrive(
+                    wall.at[row_y, 2 * row_z + row_x, oc], sem_sib, (row_z, row_x, row_y)
+                )
+    for copy in sends:
+        copy.wait_send()
+
+    for row_y in range(2):
+        for row in range(8):
+            for half in range(2):
+                block = wall.at[row_y, row, half]
+                rows = slice(64 * (row % 4) + 32 * half, 64 * (row % 4) + 32 * half + 32)
+                for j in range(3):
+                    cols = slice(384 * row_y + 128 * j, 384 * row_y + 128 * j + 128)
+                    proj[row // 4, rows, cols] = block[ROW_CONV + 32 * j : ROW_CONV + 32 * j + 32]
+                outp[row // 4, rows, 128 * row_y : 128 * row_y + 128] = block[672:704]
+
+    def time_tile(layer):
+        rows = []
+        for row in range(4 * layer, 4 * layer + 4):
+            for half in range(2):
+                rows.append(
+                    jnp.concatenate(
+                        [wall[0, row, half, 704:736, :], wall[1, row, half, 704:736, :]], 1
+                    )
+                )
+        return jnp.concatenate(rows, 0)
+
+    def conv_tile(kernel, tap):
+        rows = []
+        for row, half, offset, size in tap_pieces(tap):
+            block = (2 * kernel + row, half)
+            rows.append(
+                jnp.concatenate(
+                    [
+                        wall[(0,) + block + (slice(offset, offset + size),)],
+                        wall[(1,) + block + (slice(offset, offset + size),)],
+                    ],
+                    1,
+                )
+            )
+        return rows[0] if len(rows) == 1 else jnp.concatenate(rows, 0)
+
+    embed = embed_ref[...]
+    time_pre = [dot_nn(embed, time_tile(layer))[0:1] for layer in range(2)]
+    time_bias = [pre * jax.nn.sigmoid(pre) for pre in time_pre]
+    gain = [gains_ref[k : k + 1, :] for k in range(7)]
+    column = lax.broadcasted_iota(jnp.int32, (1, D), 1)
+    heads = [
+        jnp.where(column // 64 == h, 1.0, 0.0).astype(jnp.bfloat16) for h in range(HEADS)
+    ]
+    pixel_x = lax.broadcasted_iota(jnp.int32, (256, 1), 0) % SIDE
+    not_left = jnp.where(pixel_x != 0, 1.0, 0.0)
+    not_right = jnp.where(pixel_x != SIDE - 1, 1.0, 0.0)
+
+    def put_shifts(dst, bases, values):
+        for k, base in enumerate(bases):
+            frame = values[256 * k : 256 * k + 256]
+            rows = pl.ds(base, 256)
+            dst[0, rows, :] = low(pltpu.roll(frame, 1, 0) * not_left)
+            dst[1, rows, :] = low(frame)
+            dst[2, rows, :] = low(pltpu.roll(frame, 255, 0) * not_right)
+
+    def aligned(value, multiple):
+        return value if isinstance(value, int) else pl.multiple_of(value, multiple)
+
+    def shifted(src, bases, dy, dx):
+        return jnp.concatenate(
+            [src[dx, pl.ds(aligned(base + 16 * (dy - 1), 16), 256), :] for base in bases], 0
+        )
+
+    def conv(src, bases, kernel):
+        total = None
+        for tap in range(9):
+            part = dot_nn(shifted(src, bases, tap // 3, tap % 3), conv_tile(kernel, tap))
+            total = part if total is None else total + part
+        return total
+
+    def conv_back(src, bases, kernel):
+        total = None
+        for tap in range(9):
+            part = dot_nt(shifted(src, bases, 2 - tap // 3, 2 - tap % 3), conv_tile(kernel, tap))
+            total = part if total is None else total + part
+        return total
+
+    def conv_grad(act, src, kernel, dst, first_row):
+        for tap in range(9):
+            grads = shifted(src, [16 + GAP * k for k in range(8)], 2 - tap // 3, 2 - tap % 3)
+            total = low(dot_nn(act[...], grads))
+            start = 0
+            for row, half, offset, size in tap_pieces(tap):
+                for row_y in range(2):
+                    dst[row_y, first_row + row, half, offset : offset + size] = total[
+                        start : start + size, 128 * row_y : 128 * row_y + 128
+                    ]
+                start += size
+
+    def put_proj_grad(layer, din, dout, dst, first_row):
+        for row in range(4):
+            for half in range(2):
+                rows = slice(64 * row + 32 * half, 64 * row + 32 * half + 32)
+                for row_y in range(2):
+                    for j in range(3):
+                        cols = slice(384 * row_y + 128 * j, 384 * row_y + 128 * j + 128)
+                        dst[
+                            row_y,
+                            first_row + row,
+                            half,
+                            ROW_CONV + 32 * j : ROW_CONV + 32 * j + 32,
+                        ] = din[rows, cols]
+                    dst[row_y, first_row + row, half, 672:704] = dout[
+                        rows, 128 * row_y : 128 * row_y + 128
+                    ]
+
+    def softmax(scores):
+        powers = jnp.exp(scores - jnp.max(scores, -1, keepdims=True))
+        return low(powers * (1.0 / jnp.sum(powers, -1, keepdims=True)))
+
+    def attend(query, key, value, bias):
+        probs = []
+        for h in range(HEADS):
+            scores = dot_nt(query * heads[h], key) * 0.125
+            if bias is not None:
+                scores = scores + bias[h]
+            probs.append(softmax(scores))
+        values = jnp.concatenate([value * heads[h] for h in range(HEADS)], 0)
+        return low(dot_nn(jnp.concatenate(probs, 1), values)), probs
+
+    def attend_back(query, key, value, dmix, probs, add_bias):
+        dmix_t, query_t = dmix.T, query.T
+        dscores, dkey_t, dvalue_t = [], [], []
+        for h in range(HEADS):
+            prob_low = probs(h)
+            prob = prob_low.astype(jnp.float32)
+            dprob = dot_nt(dmix * heads[h], value)
+            dscore = prob * (dprob - jnp.sum(prob * dprob, -1, keepdims=True))
+            if add_bias is not None:
+                add_bias(h, dscore)
+            dscore_low = low(dscore)
+            dscores.append(dscore_low)
+            rows = slice(64 * h, 64 * h + 64)
+            dvalue_t.append(dot_nn(dmix_t[rows], prob_low))
+            dkey_t.append(dot_nn(query_t[rows], dscore_low))
+        keys = jnp.concatenate([key * heads[h] for h in range(HEADS)], 0)
+        dquery = low(dot_nn(jnp.concatenate(dscores, 1), keys) * 0.125)
+        dkey = low(jnp.concatenate(dkey_t, 0) * 0.125).T
+        dvalue = low(jnp.concatenate(dvalue_t, 0)).T
+        return jnp.concatenate([dquery, dkey, dvalue], 1)
+
+    def add_row(row, value):
+        vec_acc[row : row + 1, :] += value
+
+    def embed_input(rows):
+        clip = clip_ref[rows, :]
+        total = None
+        for channel in range(3):
+            part = clip[:, 3 + channel : 4 + channel] * win_ref[channel : channel + 1, :]
+            total = part if total is None else total + part
+        return total, clip
+
+    fwd_bases = [16, 16 + GAP]
+
+    def pair_rows(pair):
+        return pl.ds(pl.multiple_of(pair * 512, 512), 512)
+
+    def pair_bases(pair):
+        return [
+            pl.multiple_of(16 + GAP * (2 * pair), 16),
+            pl.multiple_of(16 + GAP * (2 * pair + 1), 16),
+        ]
+
+    def send_pair(pair, dst, sems):
+        for k, (peer, part) in enumerate(group):
+            remote(
+                stage.at[pl.ds(32 * pair + 8 * part, 8)],
+                dst.at[:, 4 * quarter + pair],
+                sems,
+                (pair, k),
+                (pair, k),
+                peer,
+            ).start()
+        dst[:, 4 * quarter + pair] = stage[pl.ds(32 * pair + 8 * quarter, 8)]
+
+    def wait_pairs(dst, sems):
+        for pair in range(PAIRS):
+            for k, (peer, part) in enumerate(group):
+                copy = remote(
+                    stage.at[pl.ds(32 * pair + 8 * part, 8)],
+                    dst.at[:, 4 * part + pair],
+                    sems,
+                    (pair, k),
+                    (pair, k),
+                    peer,
+                )
+                copy.wait_send()
+                copy.wait_recv()
+
+    def block_tiles(src, block, part):
+        return src.at[pl.ds(16 * block + 4 * part, 4)]
+
+    def send_block(block, src, dst, sems):
+        for k, (peer, part) in enumerate(group):
+            remote(
+                block_tiles(src, block, part),
+                dst.at[:, quarter, block],
+                sems,
+                (block, k),
+                (block, k),
+                peer,
+            ).start()
+        dst[:, quarter, block] = block_tiles(src, block, quarter)[...]
+
+    def wait_blocks(src, dst, sems):
+        for block in range(8):
+            for k, (peer, part) in enumerate(group):
+                copy = remote(
+                    block_tiles(src, block, part),
+                    dst.at[:, part, block],
+                    sems,
+                    (block, k),
+                    (block, k),
+                    peer,
+                )
+                copy.wait_send()
+                copy.wait_recv()
+
+    def forward_pair(pair, carry):
+        rows = pair_rows(pair)
+        hidden, _ = embed_input(rows)
+        normed, _ = rms(hidden, gain[0])
+        put_shifts(shift_fwd, fwd_bases, normed * jax.nn.sigmoid(normed))
+        inner = conv(shift_fwd, fwd_bases, 0) + time_bias[0]
+        inner_zero[rows, :] = inner
+        normed, _ = rms(inner, gain[1])
+        put_shifts(shift_fwd, fwd_bases, normed * jax.nn.sigmoid(normed))
+        hidden = hidden + conv(shift_fwd, fwd_bases, 1)
+        hid_one[rows, :] = hidden
+        normed, _ = rms(hidden, gain[2])
+        packed = low(dot_nn(low(normed), proj[0]))
+        pack_zero[rows, :] = packed
+        mixed = []
+        for k in range(2):
+            part = packed[256 * k : 256 * k + 256]
+            one, _ = attend(part[:, :D], part[:, D : 2 * D], part[:, 2 * D :], None)
+            mixed.append(one)
+        mixed = jnp.concatenate(mixed, 0)
+        mix_zero[rows, :] = mixed
+        hidden = hidden + dot_nn(mixed, outp[0])
+        hid_two[rows, :] = hidden
+        normed, _ = rms(hidden, gain[3])
+        stage[pl.ds(32 * pair, 32)] = low(weave(normed)).reshape(32, 16, D)
+        send_pair(pair, spread_norm, sem_n)
+        return carry
+
+    lax.fori_loop(0, PAIRS, forward_pair, 0)
+    wait_pairs(spread_norm, sem_n)
+
+    def temporal_block(block, carry):
+        normed = spread_norm[block].reshape(256, D)
+        packed = low(dot_nn(normed, proj[1]))
+        pack_one[block] = packed
+        mixed, probs = attend(
+            packed[:, :D],
+            packed[:, D : 2 * D],
+            packed[:, 2 * D :],
+            [table_ref[h] for h in range(HEADS)],
+        )
+        for h in range(HEADS):
+            prob_one[block, h] = probs[h]
+        mix_one[pl.ds(16 * block, 16)] = mixed.reshape(16, 16, D)
+        send_block(block, mix_one, mix_back, sem_m)
+        return carry
+
+    lax.fori_loop(0, 8, temporal_block, 0)
+    wait_blocks(mix_one, mix_back, sem_m)
+
+    scale = scal_ref[0]
+
+    def last_pair(pair, carry):
+        rows = pair_rows(pair)
+        bases = pair_bases(pair)
+        lanes = pl.ds(pl.multiple_of(pair * 512, 512), 512)
+        hidden = hid_two[rows, :] + unweave(dot_nn(mix_back[pair].reshape(512, D), outp[1]))
+        normed, inverse = rms(hidden, gain[4])
+        sig = jax.nn.sigmoid(normed)
+        acts = normed * sig
+        put_shifts(shift_fwd, fwd_bases, acts)
+        act_one[:, lanes] = low(acts).T
+        slope_one = sig * (1.0 + normed * (1.0 - sig))
+        inner = conv(shift_fwd, fwd_bases, 2) + time_bias[1]
+        normed_two, inverse_two = rms(inner, gain[5])
+        sig_two = jax.nn.sigmoid(normed_two)
+        acts_two = normed_two * sig_two
+        put_shifts(shift_fwd, fwd_bases, acts_two)
+        act_two[:, lanes] = low(acts_two).T
+        slope_two = sig_two * (1.0 + normed_two * (1.0 - sig_two))
+        last = hidden + conv(shift_fwd, fwd_bases, 3)
+        normed, inverse_six = rms(last, gain[6])
+        normed_low = low(normed)
+        pred = dot_nt(normed_low, headpad_ref[...])
+        clip = clip_ref[rows, :]
+        valid = jnp.concatenate(
+            [
+                jnp.full((256, 128), scal_ref[1 + 2 * pair], jnp.float32),
+                jnp.full((256, 128), scal_ref[2 + 2 * pair], jnp.float32),
+            ],
+            0,
+        )
+        lane = lax.broadcasted_iota(jnp.int32, (512, 128), 1)
+        error = jnp.where(lane < 3, pred - clip, 0.0)
+        weighted = error * valid
+        vec_acc[7:8, 0:128] += jnp.sum(weighted * error, 0, keepdims=True)
+        dpred = weighted * scale
+        dpred_hi = low(dpred)
+        dpred_lo = low(dpred - dpred_hi.astype(jnp.float32))
+        acc_out[...] += dot_tn(dpred_hi, normed_low) + dot_tn(dpred_lo, normed_low)
+        dnormed = None
+        for channel in range(3):
+            part = dpred[:, channel : channel + 1] * wout_ref[channel : channel + 1, :]
+            dnormed = part if dnormed is None else dnormed + part
+        dlast, dgain = rms_back(last, inverse_six, gain[6], dnormed)
+        add_row(6, dgain)
+        put_shifts(shift_two, bases, low(dlast).astype(jnp.float32))
+        dnormed = conv_back(shift_two, bases, 3) * slope_two
+        dinner, dgain = rms_back(inner, inverse_two, gain[5], dnormed)
+        add_row(5, dgain)
+        add_row(15, jnp.sum(dinner, 0, keepdims=True))
+        put_shifts(shift_one, bases, low(dinner).astype(jnp.float32))
+        dnormed = conv_back(shift_one, bases, 2) * slope_one
+        dhidden, dgain = rms_back(hidden, inverse, gain[4], dnormed)
+        add_row(4, dgain)
+        dhidden = dhidden + dlast
+        dhid[rows, :] = dhidden
+        stage[pl.ds(32 * pair, 32)] = low(weave(dhidden)).reshape(32, 16, D)
+        send_pair(pair, dout_pix, sem_dy)
+        return carry
+
+    lax.fori_loop(0, PAIRS, last_pair, 0)
+    conv_grad(act_two, shift_two, 3, wall, 6)
+    conv_grad(act_one, shift_one, 2, wall, 4)
+    wait_pairs(dout_pix, sem_dy)
+
+    def temporal_back(block, carry):
+        dout = dout_pix[block].reshape(256, D)
+        dmix = low(dot_nt(dout, outp[1]))
+        packed = pack_one[block]
+
+        def add_bias(h, dscore):
+            bias_acc[h] += dscore
+
+        dpacked = attend_back(
+            packed[:, :D],
+            packed[:, D : 2 * D],
+            packed[:, 2 * D :],
+            dmix,
+            lambda h: prob_one[block, h],
+            add_bias,
+        )
+        pack_one[block] = dpacked
+        stage[pl.ds(16 * block, 16)] = low(dot_nt(dpacked, proj[1])).reshape(16, 16, D)
+        send_block(block, stage, dnorm_back, sem_dn)
+        return carry
+
+    lax.fori_loop(0, 8, temporal_back, 0)
+    flat = (2048, D)
+    dout_one = low(dot_tn(mix_one[...].reshape(flat), dout_pix[...].reshape(flat)))
+    din_one = low(dot_tn(spread_norm[...].reshape(flat), pack_one[...].reshape(2048, 3 * D)))
+    put_proj_grad(1, din_one, dout_one, wall, 4)
+    wait_blocks(stage, dnorm_back, sem_dn)
+
+    def slab(k):
+        return (wall, 2 * k) if k >= 2 else (dslab, 2 * k)
+
+    top, low_half = pl.ds(0, HALF), pl.ds(HALF, HALF)
+
+    def red_one(k):
+        src, row = slab(k)
+        return remote(
+            src.at[:, pl.ds(row, 2), oc, pl.ds(0, ROW_GRAD)], red_sib.at[k], sem_red, (k, 0), (k, 0), sibling
+        )
+
+    def red_two(k):
+        src, row = slab(k)
+        return (
+            remote(src.at[:, row + ox, c, top], red_a.at[k], sem_red, (k, 1), (k, 1), x_peer),
+            remote(src.at[oy, pl.ds(row, 2), c, low_half], red_b.at[k], sem_red, (k, 2), (k, 2), y_peer),
+        )
+
+    def red_three(k):
+        src, row = slab(k)
+        return (
+            remote(src.at[oy, row + x, c, top], red_c.at[k], sem_red, (k, 3), (k, 3), y_peer),
+            remote(src.at[y, row + ox, c, low_half], red_d.at[k], sem_red, (k, 4), (k, 4), x_peer),
+        )
+
+    def both(left, right):
+        return low(left.astype(jnp.float32) + right.astype(jnp.float32))
+
+    def finish(copies):
+        for copy in copies:
+            copy.wait_send()
+            copy.wait_recv()
+
+    def add_one(k):
+        src, row = slab(k)
+        for row_y in range(2):
+            for row_x in range(2):
+                src[row_y, row + row_x, c, 0:ROW_GRAD] = both(
+                    src[row_y, row + row_x, c, 0:ROW_GRAD], red_sib[k, row_y, row_x]
+                )
+
+    def add_two(k):
+        src, row = slab(k)
+        for part in range(2):
+            src[part, row + x, c, 0:HALF] = both(src[part, row + x, c, 0:HALF], red_a[k, part])
+            src[y, row + part, c, HALF:ROW_GRAD] = both(
+                src[y, row + part, c, HALF:ROW_GRAD], red_b[k, part]
+            )
+
+    def add_three(k):
+        src, row = slab(k)
+        part_z[k, 0:HALF] = both(src[y, row + x, c, 0:HALF], red_c[k])
+        part_z[k, HALF:ROW_GRAD] = both(src[y, row + x, c, HALF:ROW_GRAD], red_d[k])
+
+    def start_all(copies):
+        for copy in copies:
+            copy.start()
+
+    def spatial_back(pair, carry):
+        rows = pair_rows(pair)
+        bases = pair_bases(pair)
+        lanes = pl.ds(pl.multiple_of(pair * 512, 512), 512)
+        dnormed = unweave(dnorm_back[pair].reshape(512, D).astype(jnp.float32))
+        hidden = hid_two[rows, :]
+        _, inverse = rms(hidden, gain[3])
+        dhidden, dgain = rms_back(hidden, inverse, gain[3], dnormed)
+        add_row(3, dgain)
+        dhidden = dhidden + dhid[rows, :]
+        grad_low = low(dhidden)
+        dout_pix[pl.ds(2 * pair, 2)] = grad_low.reshape(2, 16, 16, D)
+        dmix = low(dot_nt(grad_low, outp[0]))
+        packed = pack_zero[rows, :]
+        dpacked = []
+        for k in range(2):
+            part = packed[256 * k : 256 * k + 256]
+            query, key, value = part[:, :D], part[:, D : 2 * D], part[:, 2 * D :]
+
+            def again(h):
+                return softmax(dot_nt(query * heads[h], key) * 0.125)
+
+            dpacked.append(
+                attend_back(query, key, value, dmix[256 * k : 256 * k + 256], again, None)
+            )
+        dpacked = jnp.concatenate(dpacked, 0)
+        pack_zero[rows, :] = dpacked
+        hidden = hid_one[rows, :]
+        normed, inverse = rms(hidden, gain[2])
+        spread_norm[pl.ds(2 * pair, 2)] = low(normed).reshape(2, 16, 16, D)
+        dnormed = dot_nt(dpacked, proj[0])
+        dprev, dgain = rms_back(hidden, inverse, gain[2], dnormed)
+        add_row(2, dgain)
+        dhidden = dhidden + dprev
+        dhid[rows, :] = dhidden
+        put_shifts(shift_two, bases, low(dhidden).astype(jnp.float32))
+        normed, _ = rms(inner_zero[rows, :], gain[1])
+        act_two[:, lanes] = low(normed * jax.nn.sigmoid(normed)).T
+        return carry
+
+    start_all([red_one(3), red_one(2)])
+    lax.fori_loop(0, PAIRS, spatial_back, 0)
+    for k in (3, 2):
+        finish([red_one(k)])
+        add_one(k)
+        start_all(red_two(k))
+    din_zero = low(dot_tn(spread_norm[...].reshape(flat), pack_zero[...]))
+    dout_zero = low(dot_tn(mix_zero[...], dout_pix[...].reshape(flat)))
+    put_proj_grad(0, din_zero, dout_zero, dslab, 0)
+    conv_grad(act_two, shift_two, 1, dslab, 2)
+    start_all([red_one(1)])
+    for k in (3, 2):
+        finish(red_two(k))
+        add_two(k)
+        start_all(red_three(k))
+
+    def first_back(pair, carry):
+        rows = pair_rows(pair)
+        bases = pair_bases(pair)
+        lanes = pl.ds(pl.multiple_of(pair * 512, 512), 512)
+        inner = inner_zero[rows, :]
+        normed, inverse = rms(inner, gain[1])
+        sig = jax.nn.sigmoid(normed)
+        dnormed = conv_back(shift_two, bases, 1) * (sig * (1.0 + normed * (1.0 - sig)))
+        dinner, dgain = rms_back(inner, inverse, gain[1], dnormed)
+        add_row(1, dgain)
+        add_row(14, jnp.sum(dinner, 0, keepdims=True))
+        put_shifts(shift_one, bases, low(dinner).astype(jnp.float32))
+        hidden, _ = embed_input(rows)
+        normed, _ = rms(hidden, gain[0])
+        act_one[:, lanes] = low(normed * jax.nn.sigmoid(normed)).T
+        return carry
+
+    lax.fori_loop(0, PAIRS, first_back, 0)
+    conv_grad(act_one, shift_one, 0, dslab, 0)
+    start_all([red_one(0)])
+    for k in (3, 2):
+        finish(red_three(k))
+        add_three(k)
+    finish([red_one(1)])
+    add_one(1)
+    start_all(red_two(1))
+
+    def input_back(pair, carry):
+        rows = pair_rows(pair)
+        bases = pair_bases(pair)
+        hidden, clip = embed_input(rows)
+        normed, inverse = rms(hidden, gain[0])
+        sig = jax.nn.sigmoid(normed)
+        dnormed = conv_back(shift_one, bases, 0) * (sig * (1.0 + normed * (1.0 - sig)))
+        dhidden, dgain = rms_back(hidden, inverse, gain[0], dnormed)
+        add_row(0, dgain)
+        dhidden = dhidden + dhid[rows, :]
+        for channel in range(3):
+            add_row(
+                8 + channel,
+                jnp.sum(clip[:, 3 + channel : 4 + channel] * dhidden, 0, keepdims=True),
+            )
+        return carry
+
+    lax.fori_loop(0, PAIRS, input_back, 0)
+    finish(red_two(1))
+    add_two(1)
+    start_all(red_three(1))
+    finish([red_one(0)])
+    add_one(0)
+    start_all(red_two(0))
+
+    vec_acc[11:14, :] = acc_out[0:3, :]
+    place = 4 * (z // 2) + 2 * y + z % 2
+    fold = lax.broadcasted_iota(jnp.int32, (256, 128), 0) // 8
+    fold_lane = lax.broadcasted_iota(jnp.int32, (256, 128), 1)
+    left = jnp.where(fold == fold_lane, 1.0, 0.0)
+    table = None
+    for h in range(HEADS):
+        right = jnp.where(fold + 32 * h == fold_lane, 1.0, 0.0)
+        wide = lax.dot_general(
+            bias_acc[h], right, (((1,), (0,)), ((), ())), precision=HIGH, preferred_element_type=jnp.float32
+        )
+        part = lax.dot_general(
+            left, wide, (((0,), (0,)), ((), ())), precision=HIGH, preferred_element_type=jnp.float32
+        )
+        table = part if table is None else table + part
+    vec_acc[32:64, 0:128] = table[0:32]
+    row_ids = lax.broadcasted_iota(jnp.int32, (16, D), 0)
+    slots = jnp.zeros((16, D), jnp.float32)
+    for layer in range(2):
+        pre = time_pre[layer]
+        sig = jax.nn.sigmoid(pre)
+        dpre = vec_acc[14 + layer : 15 + layer, :] * (sig * (1.0 + pre * (1.0 - sig)))
+        slots = jnp.where(row_ids == 2 * place + layer, dpre, slots)
+    vec_acc[16:32, :] = slots
+
+    def total_step(values, received, sems, index, peers):
+        copies = [
+            remote(values, received.at[index + r], sems, (1 + index + k,), (1 + index + r,), peer)
+            for k, r, peer in peers
+        ]
+        start_all(copies)
+        finish(copies)
+
+    def total_pair(values, received, sems, index, peer):
+        total_step(values, received, sems, index, [(0, 0, peer)])
+        values[...] += received[index]
+
+    def total_z(values, received, sems):
+        peers = [(k, 2 - k, peer) for k, peer in enumerate(z_peers)]
+        total_step(values, received, sems, 3, peers)
+        return (values[...] + received[4]) + (received[3] + received[5])
+
+    total_pair(vec_acc, vec_recv, sem_vec, 0, sibling)
+    finish(red_three(1))
+    add_three(1)
+    finish(red_two(0))
+    add_two(0)
+    start_all(red_three(0))
+    total_pair(vec_acc, vec_recv, sem_vec, 1, x_peer)
+    total_pair(vec_acc, vec_recv, sem_vec, 2, y_peer)
+    finish(red_three(0))
+    add_three(0)
+    z_copies = [
+        remote(part_z.at[z_ids[k]], red_z.at[2 - k], sem_fin, (k,), (2 - k,), peer)
+        for k, peer in enumerate(z_peers)
+    ]
+    start_all(z_copies)
+    vector_ref[...] = total_z(vec_acc, vec_recv, sem_vec)
+    finish(z_copies)
+    total = part_z[z].astype(jnp.float32)
+    for k in range(3):
+        total = total + red_z[k].astype(jnp.float32)
+    final[c] = total
+    own_sums = remote(final.at[c], final.at[c], sem_fin, (3,), (3,), sibling)
+    own_sums.start()
+    square = jnp.sum(jnp.sum(total * total, 0, keepdims=True), 1, keepdims=True)
+    sq_acc[...] = jnp.broadcast_to(square, (8, 128))
+    grads_ref[c] = total
+    total_pair(sq_acc, sq_recv, sem_sq, 0, sibling)
+    total_pair(sq_acc, sq_recv, sem_sq, 1, x_peer)
+    total_pair(sq_acc, sq_recv, sem_sq, 2, y_peer)
+    squares_ref[...] = total_z(sq_acc, sq_recv, sem_sq)
+    own_sums.wait_send()
+    arrive(final.at[oc], sem_fin, (3,))
+    grads_ref[oc] = final[oc]
+
+
+def lane_place(block, c):
+    wide = jnp.concatenate([block, block], -1)
+    lane = lax.broadcasted_iota(jnp.int32, wide.shape, wide.ndim - 1)
+    return jnp.where(lane // 64 == c, wide, jnp.zeros_like(wide))
+
+
+def shards_pairs(
+    clean,
+    noise,
+    timesteps,
+    frame_counts,
+    conv_weight,
+    conv_first,
+    conv_second,
+    proj_in,
+    proj_in_first,
+    proj_in_second,
+    proj_out,
+    proj_out_first,
+    proj_out_second,
+    time_weight,
+    time_first,
+    time_second,
+    in_weight,
+    in_first,
+    in_second,
+    out_weight,
+    out_first,
+    out_second,
+    gains,
+    gains_first,
+    gains_second,
+    rel_bias,
+    rel_bias_first,
+    rel_bias_second,
+):
+
+    pixels = clean.shape[4]
+    fr = lax.axis_index("frame")
+    ba = lax.axis_index("batch")
+    z, x = fr // 2, fr % 2
+    y, c = ba // 2, ba % 2
+    both = jnp.concatenate([clean[:, 0], noise[:, 0]], 2)
+    moved = []
+    for turn in range(2):
+        pairs = []
+        for sz in range(4):
+            for sx in range(2):
+                for sb in range(4):
+                    micro = sx if turn == 0 else 1 - sx
+                    dz, dx = 2 * micro + sb % 2, sz // 2
+                    dst = (2 * dz + dx) * 4 + 2 * (sb // 2) + sz % 2
+                    pairs.append(((2 * sz + sx) * 4 + sb, dst))
+        piece = jnp.where((x == 0) == (turn == 0), both[0], both[1])
+        moved.append(lax.ppermute(piece, ("frame", "batch"), pairs))
+    frames = jnp.where(
+        z < 2, jnp.concatenate(moved, 0), jnp.concatenate([moved[1], moved[0]], 0)
+    )
+    video = (z // 2) * 4 + 2 * y + z % 2
+    all_levels = timesteps.reshape(-1).astype(jnp.float32)
+    level = all_levels[video]
+    count = frame_counts.reshape(-1)[video]
+    pixel_total = jnp.sum(frame_counts).astype(jnp.float32) * pixels
+    alpha_bar = jnp.cos(0.5 * math.pi * (level + 1.0) / (TSTEPS + 1.0)) ** 2
+    noisy = jnp.sqrt(alpha_bar) * frames[:, :3] + jnp.sqrt(1.0 - alpha_bar) * frames[:, 3:]
+    clip = jnp.concatenate([frames[:, 3:], noisy], 1).transpose(0, 2, 1).reshape(-1, 6)
+    clip = jnp.pad(clip, ((0, 0), (0, 122)))
+    frame_ids = 8 * (2 * x + c) + jnp.arange(8)
+    live = (frame_ids < count).astype(jnp.float32)
+    scal = jnp.concatenate([(2.0 / pixel_total)[None], live])
+    half_width = D // 2
+    frequency = jnp.exp(-math.log(10000.0) * jnp.arange(half_width, dtype=jnp.float32) / half_width)
+    angles = all_levels[:, None] * frequency
+    embedding = jnp.concatenate([jnp.sin(angles), jnp.cos(angles)], -1).astype(jnp.bfloat16)
+    embed = jnp.broadcast_to(embedding[video][None], (16, D))
+    offsets = jnp.arange(FRAMES)
+    distance = offsets[None, :] - offsets[:, None]
+    bucket = jnp.minimum(jnp.abs(distance), 15) + 16 * (distance > 0).astype(jnp.int32)
+    onehot = (bucket[:, :, None] == jnp.arange(rel_bias.shape[1])[None, None, :]).astype(
+        jnp.float32
+    )
+    bias_mat = jnp.einsum("hk,lmk->hlm", rel_bias, onehot, precision=HIGH)
+    place = jnp.arange(256)
+    usable = (place[:, None] % 8 == place[None, :] % 8) & (place[None, :] // 8 < count)
+    table = jnp.where(usable, jnp.repeat(jnp.repeat(bias_mat, 8, 1), 8, 2), NEVER)
+    narrow = jnp.concatenate(
+        [
+            low(conv_weight).reshape(2, 576, 64),
+            low(proj_out).reshape(2, 32, 64),
+            low(time_weight).reshape(2, 32, 64),
+        ],
+        1,
+    )
+    narrow = lane_place(narrow, c)
+    wide = low(proj_in)
+    wide = jnp.where(
+        c == 0, jnp.pad(wide, ((0, 0), (0, 192))), jnp.pad(wide, ((0, 0), (192, 0)))
+    )
+    wide = wide.reshape(2, 32, 3, 128).transpose(0, 2, 1, 3).reshape(2, 96, 128)
+    packed = jnp.concatenate([narrow[:, :576], wide, narrow[:, 576:]], 1)
+    out_low = low(out_weight)
+    headpad = jnp.pad(out_low, ((0, 125), (0, 0)))
+    win = jnp.pad(in_weight, ((0, 5), (0, 0)))
+    wout = jnp.pad(out_low.astype(jnp.float32), ((0, 5), (0, 0)))
+    gain_rows = jnp.pad(gains, ((0, 1), (0, 0)))
+
+    bf16, f32 = jnp.bfloat16, jnp.float32
+    vmem = pl.BlockSpec(memory_space=pltpu.VMEM)
+    smem = pl.BlockSpec(memory_space=pltpu.SMEM)
+    scratch = [
+        pltpu.VMEM((2, 8, 2, ROW_ALL, 128), bf16),
+        pltpu.VMEM((2, 4, 2, ROW_GRAD, 128), bf16),
+        pltpu.VMEM((2, D, 3 * D), bf16),
+        pltpu.VMEM((2, D, D), bf16),
+        pltpu.VMEM((ROW_ALL, 128), bf16),
+        pltpu.VMEM((2048, D), f32),
+        pltpu.VMEM((2048, D), f32),
+        pltpu.VMEM((2048, D), f32),
+        pltpu.VMEM((2048, D), f32),
+        pltpu.VMEM((2048, 3 * D), bf16),
+        pltpu.VMEM((2048, D), bf16),
+        pltpu.VMEM((8, 16, 16, D), bf16),
+        pltpu.VMEM((8, 256, 3 * D), bf16),
+        pltpu.VMEM((8, HEADS, 256, 256), bf16),
+        pltpu.VMEM((128, 16, D), bf16),
+        pltpu.VMEM((PAIRS, 4, 8, 16, D), bf16),
+        pltpu.VMEM((8, 16, 16, D), bf16),
+        pltpu.VMEM((PAIRS, 4, 8, 16, D), bf16),
+        pltpu.VMEM((128, 16, D), bf16),
+        pltpu.VMEM((HEADS, 256, 256), f32),
+        pltpu.VMEM((3, 2 * GAP + 16, D), bf16),
+        pltpu.VMEM((3, 8 * GAP + 16, D), bf16),
+        pltpu.VMEM((3, 8 * GAP + 16, D), bf16),
+        pltpu.VMEM((D, 2048), bf16),
+        pltpu.VMEM((D, 2048), bf16),
+        pltpu.VMEM((128, D), f32),
+        pltpu.VMEM((4, 2, 2, ROW_GRAD, 128), bf16),
+        pltpu.VMEM((4, 2, HALF, 128), bf16),
+        pltpu.VMEM((4, 2, HALF, 128), bf16),
+        pltpu.VMEM((4, HALF, 128), bf16),
+        pltpu.VMEM((4, HALF, 128), bf16),
+        pltpu.VMEM((3, ROW_GRAD, 128), bf16),
+        pltpu.VMEM((4, ROW_GRAD, 128), bf16),
+        pltpu.VMEM((2, ROW_GRAD, 128), f32),
+        pltpu.VMEM((64, D), f32),
+        pltpu.VMEM((6, 64, D), f32),
+        pltpu.VMEM((8, 128), f32),
+        pltpu.VMEM((6, 8, 128), f32),
+        pltpu.SemaphoreType.DMA((2, 4, 2, 2)),
+        pltpu.SemaphoreType.DMA((2, 3)),
+        pltpu.SemaphoreType.DMA((2, 4)),
+        pltpu.SemaphoreType.DMA((2, 4)),
+        pltpu.SemaphoreType.DMA((2, 4)),
+        pltpu.SemaphoreType.DMA((2, 4)),
+        pltpu.SemaphoreType.DMA((2, PAIRS, 3)),
+        pltpu.SemaphoreType.DMA((2, 8, 3)),
+        pltpu.SemaphoreType.DMA((2, PAIRS, 3)),
+        pltpu.SemaphoreType.DMA((2, 8, 3)),
+        pltpu.SemaphoreType.DMA((2, 4, 5)),
+        pltpu.SemaphoreType.DMA((2, 4)),
+        pltpu.SemaphoreType.DMA((2, 8)),
+        pltpu.SemaphoreType.DMA((2, 8)),
+    ]
+    sums, vector, squares = pl.pallas_call(
+        step_kernel,
+        out_shape=(
+            jax.ShapeDtypeStruct((2, ROW_GRAD, 128), f32),
+            jax.ShapeDtypeStruct((64, D), f32),
+            jax.ShapeDtypeStruct((8, 128), f32),
+        ),
+        in_specs=[vmem] * 8 + [smem],
+        out_specs=(vmem, vmem, vmem),
+        scratch_shapes=scratch,
+        compiler_params=pltpu.CompilerParams(
+            collective_id=0, has_side_effects=True, vmem_limit_bytes=64 * 2**20 - 2**16
+        ),
+        name="train_step",
+    )(packed, clip, embed, table, gain_rows, win, wout, headpad, scal)
+
+    conv_sum = lax.dynamic_slice_in_dim(sums[:, :576].reshape(1152, 128), 64 * c, 64, 1)
+    pin_sum = sums[:, 576:672].reshape(2, 3, 32, 128).transpose(0, 2, 1, 3).reshape(64, 384)
+    pin_sum = lax.dynamic_slice_in_dim(pin_sum, 192 * c, 192, 1)
+    pout_sum = lax.dynamic_slice_in_dim(sums[:, 672:704].reshape(64, 128), 64 * c, 64, 1)
+    dpre = vector[16:32].reshape(8, 2, D)
+    dtime = jnp.einsum("vd,vje->jde", embedding.astype(f32), dpre, precision=HIGH)
+    time_square = jnp.sum(dtime * dtime)
+    time_sum = lax.dynamic_slice(dtime.reshape(2 * D, D), (64 * fr, 64 * ba), (64, 64))
+    loss_sum = jnp.sum(vector[7, :3])
+    sum_gains, sum_in, sum_out = vector[0:7], vector[8:11], vector[11:14]
+    folded = vector[32:64, :128].reshape(FRAMES, HEADS, FRAMES)
+    sum_table = jnp.einsum("lhm,lmk->hk", folded, onehot, precision=HIGH)
+    square = (
+        squares[0, 0]
+        + time_square
+        + sum((jnp.sum(grad * grad) for grad in (sum_in, sum_out, sum_gains, sum_table)))
+    )
+    grad_norm = jnp.sqrt(square)
+    clip_scale = CLIP / jnp.maximum(grad_norm, CLIP)
+    return (
+        loss_sum,
+        pixel_total,
+        grad_norm,
+        *adamw(conv_weight, conv_first, conv_second, conv_sum, clip_scale, RATES[0]),
+        *adamw(proj_in, proj_in_first, proj_in_second, pin_sum, clip_scale, RATES[1]),
+        *adamw(proj_out, proj_out_first, proj_out_second, pout_sum, clip_scale, RATES[2]),
+        *adamw(time_weight, time_first, time_second, time_sum, clip_scale, RATES[3]),
+        *adamw(in_weight, in_first, in_second, sum_in, clip_scale, RATES[4]),
+        *adamw(out_weight, out_first, out_second, sum_out, clip_scale, RATES[5]),
+        *adamw(gains, gains_first, gains_second, sum_gains, clip_scale, RATES[6]),
+        *adamw(rel_bias, rel_bias_first, rel_bias_second, sum_table, clip_scale, RATES[7]),
+    )
 
 
 def shards(
@@ -552,4 +1594,6 @@
         P(),
         P(),
     )
-    return jax.shard_map(shards, mesh=mesh, in_specs=in_specs, out_specs=out_specs, check_vma=False)
+    sizes = tuple(mesh.shape[name] for name in ("frame", "batch"))
+    local = shards_pairs if sizes == (8, 4) else shards
+    return jax.shard_map(local, mesh=mesh, in_specs=in_specs, out_specs=out_specs, check_vma=False)

time: 1090 us -> 284 us (0.26)
  waiting for transfers between devices: 355 us -> 0.01 us
  Pallas kernels: 0 us -> 226 us
  local copies, waits for them, and re-layouts: 232 us -> 18.5 us
  blocking collectives: 161 us -> 0 us
  matrix products: 155 us -> 3.28 us
  other arithmetic: 102 us -> 18.7 us
  starting transfers between devices: 49.8 us -> 7.26 us
  between operations: 28.5 us -> 9.03 us
    reduce_scatter x5 -> x0, waiting for transfers between devices: 304 us -> none  [the longest x1 159 us: reduce_rows(): lax.psum_scatter(matrix_grads[0], 'frame', scatter_dimension=0, tiled=True)]
    pallas_call x0 -> x1, Pallas kernels: none -> 226 us  [shards_pairs(): pl.pallas_call(step_kernel, out_shape=(jax.ShapeDtypeStruct((2, ROW_GRAD,...]
    dot_general x87 -> x3, matrix products: 144 us -> 3.28 us  [the longest x1 1.18 us: shards_pairs(): bias_mat = jnp.einsum('hk,lmk->hlm', rel_bias, onehot, precision=HIGH)]
    all_gather x7 -> x0, blocking collectives: 121 us -> none  [the longest x1 32.5 us: fetch(): lax.all_gather(columns[2], 'frame', axis=0, tiled=True)]
    unnamed x657 -> x85, local copies, waits for them, and re-layouts: 103 us -> 6.6 us
    all_to_all x8 -> x0, starting transfers between devices: 48.4 us -> none  [the longest x2 12.3 us: mixer_bwd(): lax.all_to_all(from_rows(dpacked, videos), 'frame', split_axis=0, concat_...]
    unnamed x12 -> x0, waiting for transfers between devices: 44.4 us -> none
    psum x1 -> x0, blocking collectives: 39.9 us -> none  [shards(): lax.psum((vector_acc[0], vector_acc[1], vector_acc[2], vector_acc[3], los...]
  transfers between devices with their start and end apart: 17 -> 2, of which waited for: 9 -> 0; matrix products, arithmetic and copies ran while one was open for 32% -> 5% of each run, Pallas kernels for 0% -> 0%
where the time goes in v1:
time: 284 us; the launch traced here: 283 us
  Pallas kernels  226 us (80%)
  other arithmetic  18.7 us (7%)
  local copies, waits for them, and re-layouts  18.5 us (7%)
  between operations  9.03 us (3%)
  starting transfers between devices  7.26 us (3%)
  matrix products  3.28 us (1%)
    pallas_call x1, Pallas kernels, shards_pairs(): pl.pallas_call(step_kernel, out_shape=(jax.ShapeDtypeStruct((2, ROW_GRAD,...  226 us
    ppermute x2, starting transfers between devices, shards_pairs(): moved.append(lax.ppermute(piece, ('frame', 'batch'), pairs))  7.26 us
    sub x7, other arithmetic, adamw(): weight - step_rate * (update + DECAY * weight)  6.68 us
    unnamed x85, local copies, waits for them, and re-layouts  6.6 us
  transfers between devices with their start and end apart: 2, of which 0 were waited for; matrix products, arithmetic and copies ran while one was open for 5% of the time, Pallas kernels for 0%

profile of v1, /device:TPU:0, one launch (start us, length us, event | category | flops | bytes accessed | tf_op | source)
XLA Modules:
  0.0 282.7 jit_solution(16965644154627927431)
XLA Ops:
  0.7 0.7 copy-done.18
  1.4 0.8 select_bitcast_fusion.1
  2.2 0.7 collective-permute-start
  2.9 6.6 %collective-permute-start.1 = (f32[4,6,256]{2,0,1:T(4,128)S(1)}, f32[4,6,256]{2,0,1:T(4,128)S(1)}, u32[]{:S(2)}, u32[]{:S(2)}) collective-permute-start(f32[4,6,256]{2,0,1:T(4,128)S(1)} %get-tuple-element.67), channel_id=1, source_target_pairs={{0,16},{1,24},{2,18},{3,26},{4,0},{5,8},{6,2},{7,10},{8,17},{9,25}... | collective-permute-start | bytes 73736 | tf_op jit(solution)/shard_map/ppermute | solution.py:1173
  9.5 1.0 convert_element_type.49
  11.3 0.8 copy-done.8
  12.3 0.7 copy-done
  13.7 1.3 fusion.27
  15.6 0.7 fusion.22
  16.3 1.2 convolution_bitcast_fusion
  21.5 1.1 broadcast_select_fusion.table_ref
  22.8 0.8 pad_maximum_fusion.packed_ref
  28.0 1.0 pad.31.clip_ref
  29.6 225.9 %train_step.1 = (f32[2,704,128]{2,1,0:T(8,128)}, f32[64,256]{1,0:T(8,128)}, f32[8,128]{1,0:T(8,128)}) custom-call(bf16[2,736,128]{2,1,0:T(8,128)(2,1)} %pad_maximum_fusion.packed_ref, f32[2048,128]{1,0:T(8,128)} %pad.31.clip_ref, bf16[16,256]{1,0:T(8,128)(2,1)} %broadcast_in_dim.38.embed_ref, f32[4,256,256]{2,1,0:T(8,128)} %broadcast_select_fusion.table_ref, ...), custom_call_target="tpu_custom_call" | custom-call | tf_op jit(solution)/shard_map/train_step/pallas_call | solution.py:1282
  255.6 1.4 multiply_reduce_fusion.1
  257.0 1.3 multiply_reduce_fusion
  258.3 0.7 slice.63
  259.0 0.7 slice.59
  259.7 0.8 slice.66
  260.5 0.9 slice.65
  261.4 1.1 slice.64
  262.5 1.3 slice_reduce_fusion
  264.5 1.0 multiply_reduce_fusion.3
  265.5 0.7 copy-done.20
  266.2 1.1 fusion.1
  267.3 1.2 slice.58
  273.5 1.4 add_subtract_fusion
  275.5 0.7 multiply_subtract_fusion.3
  276.3 1.1 multiply_subtract_fusion
  277.4 1.4 multiply_subtract_fusion.4
  278.9 0.8 multiply_subtract_fusion.1
  279.7 0.7 multiply_subtract_fusion.2
  (130 shorter events, 12.3 us)
Async XLA Ops:
  0.7 0.7 copy-start.18
  2.2 25.3 %collective-permute-start = (f32[4,6,256]{2,0,1:T(4,128)S(1)}, f32[4,6,256]{2,0,1:T(4,128)S(1)}, u32[]{:S(2)}, u32[]{:S(2)}) collective-permute-start(f32[4,6,256]{2,0,1:T(4,128)S(1)} %get-tuple-element.66), channel_id=1, source_target_pairs={{0,0},{1,8},{2,2},{3,10},{4,16},{5,24},{6,18},{7,26},{8,1},{9,9},{... | collective-permute-start | bytes 73736 | tf_op jit(solution)/shard_map/ppermute | solution.py:1173
  2.9 24.7 %collective-permute-start.1 = (f32[4,6,256]{2,0,1:T(4,128)S(1)}, f32[4,6,256]{2,0,1:T(4,128)S(1)}, u32[]{:S(2)}, u32[]{:S(2)}) collective-permute-start(f32[4,6,256]{2,0,1:T(4,128)S(1)} %get-tuple-element.67), channel_id=1, source_target_pairs={{0,16},{1,24},{2,18},{3,26},{4,0},{5,8},{6,2},{7,10},{8,17},{9,25}... | collective-permute-start | bytes 73736 | tf_op jit(solution)/shard_map/ppermute | solution.py:1173
  9.5 6.8 %copy-start.27 = (s32[32,32]{1,0:T(8,128)}, s32[32,32]{1,0:T(8,128)S(1)}, u32[]{:S(2)}) copy-start(s32[32,32]{1,0:T(8,128)S(1)} %select_add_fusion) | copy-start | bytes 12292
  10.5 0.8 copy-start.6
  11.3 0.8 copy-start.8
  17.8 2.1 copy-start.4
  21.5 1.3 slice-start
  21.5 1.3 slice-start.1
  22.7 4.8 %copy-start.19 = (bf16[8,128]{1,0:T(8,128)(2,1)}, bf16[8,128]{1,0:T(8,128)(2,1)S(1)}, u32[]{:S(2)}) copy-start(bf16[8,128]{1,0:T(8,128)(2,1)S(1)} %get-tuple-element.68) | copy-start | bytes 6148
  22.7 4.8 %copy-start.21 = (bf16[8,128]{1,0:T(8,128)(2,1)}, bf16[8,128]{1,0:T(8,128)(2,1)S(1)}, u32[]{:S(2)}) copy-start(bf16[8,128]{1,0:T(8,128)(2,1)S(1)} %get-tuple-element.69) | copy-start | bytes 6148
  272.8 2.1 copy-start.36
  272.8 2.1 copy-start.37
  272.8 2.1 copy-start.38
  272.8 2.7 copy-start.7
  272.8 2.6 copy-start.12
  272.8 2.6 copy-start.13
  272.8 3.4 %copy-start.2 = (f32[1152,64]{0,1:T(8,128)S(1)}, f32[1152,64]{0,1:T(8,128)}, u32[]{:S(2)}) copy-start(f32[1152,64]{0,1:T(8,128)} %param.33) | copy-start | bytes 884740
  272.9 3.3 %copy-start.3 = (f32[1152,64]{0,1:T(8,128)S(1)}, f32[1152,64]{0,1:T(8,128)}, u32[]{:S(2)}) copy-start(f32[1152,64]{0,1:T(8,128)} %param.34) | copy-start | bytes 884740
  273.5 2.7 copy-start.1
  276.2 1.2 copy-start.24
  276.2 1.2 copy-start.26
  276.2 1.1 copy-start.31
  276.2 1.1 copy-start.32
  276.3 1.1 copy-start.33
  276.3 1.1 copy-start.34
  276.3 2.5 copy-start.5
  276.3 2.5 copy-start.10
  276.3 2.5 copy-start.11
  278.8 0.8 copy-start.9
  278.8 0.8 copy-start.14
  278.9 0.8 copy-start.15
  (13 other events, 9.1 us)
